TPU v7x, 256 devices: a whole 4x4x8 slice. The times are simulated.
256 devices in a mesh: member: 32 (over z, y), region: 8 (over x, core).
Axes of the slice: x: 4, y: 4, z: 8, core: 2. Of those that a mesh axis runs over, the one named last changes fastest.
Arguments:
- background_realizations: float32 [1024, 262144], P('member', 'region'), may hold values from -6 to 6
- realization_expected_data: float32 [1024, 32768], P('member', 'region'), may hold values from -6 to 6
- departure_values: float32 [1024, 32768], P('member', 'region'), may hold values from -6 to 6
- instrument_dispersion: float32 [32768], P('region'), may hold values from 0.5 to 2
- window_piece_offsets: int32 [8, 33], P('region'), may hold values from 0 to 256, as said below
- window_data_pieces: int32 [8, 32, 4], P('region'), may hold values from 0 to 39, as said below
- neighbor_piece_ids: int32 [8, 2, 4], P('region'), may hold values from 0 to 31, as said below
- coupling_indicator: int32 [8, 256, 4], P('region'), may hold values 0 or 1
Outputs:
- analysis: float32 [1024, 262144], P('member', 'region')
Inputs may be any that keep to these rules, and one draw needn't show every extreme that they name: `window_piece_offsets`: each row starts at 0, ends at 256 and rises by 1 or more at each entry; entry p lies within 3 of p * 8; in every row one patch spans exactly 14 blocks. `window_data_pieces`: entries index a region's extended observation blocks: 0 to 31 its own, then 4 received from the region before it, then 4 from the region after it; the 4 entries of a patch differ. `neighbor_piece_ids`: entries index the sending region's own observation blocks; the 4 entries of a row differ.
All inputs are finite; a program needn't handle non-finite values. No bound on the sum of `coupling_indicator` on one device may be relied on, other than what follows from the above.
Results may differ from a plain program's by a relative error of at most 0.0003.
Values sent between devices are 32-bit elements; how exact they have to be, the bound alone decides.
No kernel may reach another device: no remote copies, remote signals or barrier semaphores. Data moves between devices by JAX's collectives and lax.ppermute only.
A program may use at most 128 MiB of HBM per device.

v0:
```python
import jax
import jax.numpy as jnp
from jax import lax
from jax.sharding import PartitionSpec as P

PIECE_LENGTH = 128
OBS_PER = 4
LOCAL = 512


highest = lax.Precision.HIGHEST


def from_behind(block, axis, distance):
    devices = range(lax.axis_size(axis))
    route = [((i - distance) % len(devices), i) for i in devices]
    return lax.ppermute(block, axis, route)


def from_behind_2(block, axis, distance):
    devices = range(lax.axis_size(axis))
    route = [(i - distance, i) for i in devices if i - distance in devices]
    return lax.ppermute(block, axis, route)


def in_blocks(x, dim, length):
    before, after = (x.shape[:dim], x.shape[dim + 1 :])
    return jnp.moveaxis(x.reshape(*before, length, -1, *after), dim, 0)


def cut_rows(length, count):
    hop = length // count
    if hop >= 8:
        hop -= hop % 8
    return [hop * k for k in range(1, count)]


def laid_out(pieces, dim):
    pieces = jnp.moveaxis(pieces, 0, dim)
    shape = pieces.shape
    return pieces.reshape(*shape[:dim], shape[dim] * shape[dim + 1], *shape[dim + 2 :])


def cut_exchange(x, axis, pieces, split_dim, concat_dim):
    blocks = in_blocks(x, split_dim, lax.axis_size(axis))
    cut = max(range(1, max(2, blocks.ndim - 1)), key=lambda d: blocks.shape[d])
    gathered = []
    for piece in jnp.split(blocks, cut_rows(blocks.shape[cut], pieces), axis=cut):
        if piece.size:
            gathered.append(lax.all_to_all(piece, axis, split_axis=0, concat_axis=0, tiled=True))
    return laid_out(jnp.concatenate(gathered, axis=cut), concat_dim)


def from_neighbour(pieces, offset):
    return from_behind((pieces[0], pieces[1], pieces[2]), "region", offset)


def rim_send(piece, offset):
    return from_behind_2(piece, "member", offset)


def rim_back(piece, offset):
    return from_behind_2(piece, "member", offset)


def local_solve(expected_data, innovated, variance):
    realization_records = expected_data.shape[0]
    perturbed = expected_data - jnp.mean(expected_data, axis=0, keepdims=True)
    cov_obs = jnp.dot(
        perturbed.T, perturbed, precision=highest, preferred_element_type=jnp.float32
    ) / (realization_records - 1.0)
    cov_obs = cov_obs + jnp.diag(variance)
    factor = jnp.linalg.cholesky(cov_obs)
    weights = jax.scipy.linalg.cho_solve((factor, True), innovated.T)
    return (perturbed, weights)


def update(centred, perturbed, weights, cover_rows):
    realization_records, row_count = centred.shape
    block_rows = row_count // PIECE_LENGTH
    kalman_gain = lax.dot_general(
        centred,
        perturbed,
        (((0,), (0,)), ((), ())),
        precision=highest,
        preferred_element_type=jnp.float32,
    ) / (realization_records - 1.0)
    kalman_gain = (
        kalman_gain.reshape(block_rows, PIECE_LENGTH, OBS_PER, PIECE_LENGTH)
        * cover_rows[:, None, :, None]
    )
    kalman_gain = kalman_gain.reshape(row_count, OBS_PER * PIECE_LENGTH)
    return lax.dot_general(
        weights,
        kalman_gain,
        (((0,), (1,)), ((), ())),
        precision=highest,
        preferred_element_type=jnp.float32,
    )


def body(
    background_realizations,
    realization_expected_data,
    departure_values,
    instrument_dispersion,
    window_piece_offsets,
    window_data_pieces,
    neighbor_piece_ids,
    coupling_indicator,
):
    groups = lax.axis_size("member")
    own_index = lax.axis_index("member")
    neighbor_realization_records, variable_total = background_realizations.shape
    segment_total = variable_total // PIECE_LENGTH
    per_device = segment_total // groups
    spread = (per_device - 1) // 2
    gathered_data = realization_expected_data.shape[1] // PIECE_LENGTH
    expected_pieces = realization_expected_data.reshape(
        neighbor_realization_records, gathered_data, PIECE_LENGTH
    )
    innov_blocks = departure_values.reshape(
        neighbor_realization_records, gathered_data, PIECE_LENGTH
    )
    var_blocks = instrument_dispersion.reshape(gathered_data, PIECE_LENGTH)
    halo_rows = neighbor_piece_ids[0]

    def listed(row):
        return (
            jnp.take(expected_pieces, row, axis=1),
            jnp.take(innov_blocks, row, axis=1),
            jnp.take(var_blocks, row, axis=0),
        )

    from_before = from_neighbour(listed(halo_rows[0]), 1)
    from_after = from_neighbour(listed(halo_rows[1]), -1)
    pred_ext = jnp.concatenate([expected_pieces, from_before[0], from_after[0]], axis=1)
    innov_ext = jnp.concatenate([innov_blocks, from_before[1], from_after[1]], axis=1)
    var_ext = jnp.concatenate([var_blocks, from_before[2], from_after[2]], axis=0)
    chosen = window_data_pieces[0]
    flat_list = chosen.reshape(-1)
    send_pred = jnp.take(pred_ext, flat_list, axis=1).reshape(
        neighbor_realization_records, groups * LOCAL
    )
    send_innov = jnp.take(innov_ext, flat_list, axis=1).reshape(
        neighbor_realization_records, groups * LOCAL
    )
    expected_data, innovated = (
        lax.all_to_all(send_pred, "member", split_axis=1, concat_axis=0, tiled=True),
        lax.all_to_all(send_innov, "member", split_axis=1, concat_axis=0, tiled=True),
    )
    own_list = lax.dynamic_index_in_dim(chosen, own_index, 0, keepdims=False)
    variance = jnp.take(var_ext, own_list, axis=0).reshape(LOCAL)
    perturbed, weights = local_solve(expected_data, innovated, variance)
    bounds_row = window_piece_offsets[0]
    cover_all = coupling_indicator[0].astype(jnp.float32)
    states = cut_exchange(background_realizations, "member", 2, 1, 0)
    centred = states - jnp.mean(states, axis=0, keepdims=True)
    width = spread * PIECE_LENGTH
    own_width = per_device * PIECE_LENGTH
    head_cols = centred[:, :width]
    tail_cols = centred[:, own_width - width :]
    got_before = rim_send(tail_cols, 1)
    got_after = rim_send(head_cols, -1)
    first_block = own_index * per_device
    rim_steps = jnp.arange(spread)
    before_ids = jnp.clip(first_block - spread + rim_steps, 0, segment_total - 1)
    after_ids = jnp.clip(first_block + per_device + rim_steps, 0, segment_total - 1)
    own_cover = lax.dynamic_slice_in_dim(cover_all, first_block, per_device, 0)
    covers = jnp.concatenate(
        [
            jnp.take(cover_all, before_ids, axis=0),
            own_cover,
            jnp.take(cover_all, after_ids, axis=0),
        ],
        axis=0,
    )
    columns = jnp.concatenate([got_before, centred, got_after], axis=1)
    increments = update(columns, perturbed, weights, covers)
    for_before = increments[:, :width]
    own_inc = increments[:, width : width + own_width]
    for_after = increments[:, width + own_width :]
    head_return = rim_back(for_after, 1)
    tail_return = rim_back(for_before, -1)
    own_blocks = first_block + jnp.arange(per_device)
    owners = jnp.sum((bounds_row[None, 1:-1] <= own_blocks[:, None]).astype(jnp.int32), axis=1)
    head_mask = jnp.repeat(owners[:spread] == own_index - 1, PIECE_LENGTH)[None, :]
    tail_mask = jnp.repeat(owners[per_device - spread :] == own_index + 1, PIECE_LENGTH)[None, :]
    head_inc = jnp.where(head_mask, head_return, own_inc[:, :width])
    tail_inc = jnp.where(tail_mask, tail_return, own_inc[:, own_width - width :])
    full_inc = jnp.concatenate([head_inc, own_inc[:, width : own_width - width], tail_inc], axis=1)
    analysis = lax.all_to_all(states + full_inc, "member", split_axis=0, concat_axis=1, tiled=True)
    return analysis


def solution(mesh):
    return jax.shard_map(
        body,
        mesh=mesh,
        in_specs=(
            P("member", "region"),
            P("member", "region"),
            P("member", "region"),
            P("region"),
            P("region", None),
            P("region", None, None),
            P("region", None, None),
            P("region", None, None),
        ),
        out_specs=P("member", "region"),
        check_vma=False,
    )
```

profile of v0, /device:TPU:12, one launch (start us, length us, event | category | flops | bytes accessed | tf_op | source)
XLA Modules:
  0.0 548.3 jit_solution(3095665081516821695)
XLA Ops:
  0.0 2.6 copy.104
  2.6 1.8 fusion.82
  4.3 62.1 %all_to_all.64 = f32[32,16,1024]{2,1,0:T(8,128)} all-to-all(f32[32,16,1024]{2,1,0:T(8,128)S(1)} %get-tuple-element.38), channel_id=1, replica_groups=mesh['member'=32,'region'=8] {'member'}, dimensions={0} | all-to-all | bytes 4194304 | tf_op jit(solution)/shard_map/all_to_all | solution.py:50
  66.5 5.7 %all-to-all-start.1 = ((f32[32,16,1024]{2,1,0:T(8,128)}), f32[32,16,1024]{2,1,0:T(8,128)S(1)}, u32[]{:S(2)}, u32[]{:S(2)}) async-start(f32[32,16,1024]{2,1,0:T(8,128)} %get-tuple-element.37), calls=%async_computation.1 | async-start | bytes 4194304 | tf_op jit(solution)/shard_map/all_to_all | solution.py:50
  77.2 1.7 collective-permute-start.1
  78.9 1.7 collective-permute-start.5
  81.4 1.3 broadcast_select_fusion.3
  82.7 1.3 gather_fusion.5
  87.1 2.2 gather_fusion.3
  89.4 2.3 gather_fusion.8
  91.6 3.9 select_bitcast_fusion
  95.6 2.6 copy.77
  98.2 2.7 all_to_all.48
  100.9 4.2 copy.78
  105.1 15.6 %all-to-all-done.1 = f32[32,16,1024]{2,1,0:T(8,128)S(1)} async-done(((f32[32,16,1024]{2,1,0:T(8,128)}), f32[32,16,1024]{2,1,0:T(8,128)S(1)}, u32[]{:S(2)}, u32[]{:S(2)}) %all-to-all-start.1) | async-done | bytes 2097184 | tf_op jit(solution)/shard_map/all_to_all | solution.py:50
  120.7 1.3 copy-done.7
  122.0 6.5 %all-to-all-start.2 = ((f32[32,32,512]{2,0,1:T(8,128)}), f32[32,32,512]{2,0,1:T(8,128)S(1)}, u32[]{:S(2)}, u32[]{:S(2)}) async-start(f32[32,32,512]{2,0,1:T(8,128)} %copy.78), calls=%async_computation.2 | async-start | bytes 4194304 | tf_op jit(solution)/shard_map/all_to_all | solution.py:149
  132.1 4.1 copy.83
  136.3 2.8 all_to_all.51
  139.1 4.3 copy.84
  143.7 1.2 copy-done.8
  146.2 1.3 copy-done.3
  147.5 2.2 fusion.81
  150.4 3.4 collective-permute-start.6
  153.8 3.6 collective-permute-start.7
  157.4 19.2 %all-to-all-done.2 = f32[32,32,512]{2,0,1:T(8,128)S(1)} async-done(((f32[32,32,512]{2,0,1:T(8,128)}), f32[32,32,512]{2,0,1:T(8,128)S(1)}, u32[]{:S(2)}, u32[]{:S(2)}) %all-to-all-start.2) | async-done | bytes 2097184 | tf_op jit(solution)/shard_map/all_to_all | solution.py:149
  176.6 7.4 %all-to-all-start.3 = ((f32[32,32,512]{2,0,1:T(8,128)}), f32[32,32,512]{2,0,1:T(8,128)}, u32[]{:S(2)}, u32[]{:S(2)}) async-start(f32[32,32,512]{2,0,1:T(8,128)} %copy.84), calls=%async_computation.3 | async-start | bytes 4194304 | tf_op jit(solution)/shard_map/all_to_all | solution.py:150
  184.2 4.6 fusion.31
  188.8 2.5 copy.79
  191.3 1.8 add_multiply_fusion
  194.1 11.7 %cholesky.103 = f32[128,128]{1,0:T(8,128)S(1)} custom-call(f32[128,128]{1,0:T(8,128)S(1)} %cholesky.263), custom_call_target="Cholesky" | custom-call | tf_op jit(solution)/shard_map/jit(cholesky)/cholesky | solution.py:73
  207.0 9.8 %custom-call.34 = f32[1,128,128]{1,2,0:T(8,128)S(1)} custom-call(f32[1,128,128]{2,1,0:T(8,128)S(1)} %get-tuple-element.54), custom_call_target="InvertDiagBlocksLowerTriangular" | custom-call | tf_op jit(solution)/shard_map/jit(cholesky)/cholesky | solution.py:73
  216.8 1.9 constant_dynamic-update-slice_fusion.5
  218.7 1.2 convolution_subtract_fusion.4
  220.0 11.9 %cholesky.215 = f32[128,128]{1,0:T(8,128)S(1)} custom-call(f32[128,128]{1,0:T(8,128)S(1)} %cholesky.267), custom_call_target="Cholesky" | custom-call | tf_op jit(solution)/shard_map/jit(cholesky)/cholesky | solution.py:73
  232.6 9.8 %custom-call.35 = f32[1,128,128]{1,2,0:T(8,128)S(1)} custom-call(f32[1,128,128]{2,1,0:T(8,128)S(1)} %get-tuple-element.51), custom_call_target="InvertDiagBlocksLowerTriangular" | custom-call | tf_op jit(solution)/shard_map/jit(cholesky)/cholesky | solution.py:73
  243.3 1.4 convolution_subtract_fusion.5
  244.7 11.7 %cholesky.236 = f32[128,128]{1,0:T(8,128)S(1)} custom-call(f32[128,128]{1,0:T(8,128)S(1)} %cholesky.272), custom_call_target="Cholesky" | custom-call | tf_op jit(solution)/shard_map/jit(cholesky)/cholesky | solution.py:73
  257.1 9.8 %custom-call.36 = f32[1,128,128]{1,2,0:T(8,128)S(1)} custom-call(f32[1,128,128]{2,1,0:T(8,128)S(1)} %get-tuple-element.48), custom_call_target="InvertDiagBlocksLowerTriangular" | custom-call | tf_op jit(solution)/shard_map/jit(cholesky)/cholesky | solution.py:73
  267.7 1.4 convolution_subtract_fusion.6
  269.2 12.1 %cholesky.253 = f32[128,128]{1,0:T(8,128)S(1)} custom-call(f32[128,128]{1,0:T(8,128)S(1)} %convolution_subtract_fusion.6), custom_call_target="Cholesky" | custom-call | tf_op jit(solution)/shard_map/jit(cholesky)/cholesky | solution.py:73
  286.7 2.4 select_select_fusion
  289.0 11.9 %while.1 = (s32[]{:T(128)}, f32[512,512]{1,0:T(8,128)}, s32[4,2]{0,1:T(2,128)S(1)}, f32[4,128,128]{2,1,0:T(8,128)S(1)}, s32[]{:T(128)}) while((s32[]{:T(128)}, f32[512,512]{1,0:T(8,128)}, s32[4,2]{0,1:T(2,128)S(1)}, f32[4,128,128]{2,1,0:T(8,128)S(1)}, s32[]{:T(128)}) %tuple.49), condition=%wide.while_cond, body=%wide.while_body.sunk | while | flops 2 | bytes 131181 | solution.py:74
  289.7 2.3 bitcast_dynamic-update-slice_fusion.2
  292.7 2.3 bitcast_dynamic-update-slice_fusion.2
  295.7 2.3 bitcast_dynamic-update-slice_fusion.2
  298.7 2.2 bitcast_dynamic-update-slice_fusion.2
  301.0 39.3 %custom-call.37 = f32[4,128,128]{1,2,0:T(8,128)S(1)} custom-call(f32[4,128,128]{2,1,0:T(8,128)S(1)} %get-tuple-element.16), custom_call_target="InvertDiagBlocksLowerTriangular" | custom-call | tf_op jit(solution)/shard_map/jit(_cho_solve)/triangular_solve | solution.py:74
  340.3 3.1 copy.85
  343.4 1.8 fusion.45
  345.2 1.7 convolution_subtract_fusion.3
  353.8 1.1 fusion.32
  355.8 1.9 copy-done.6
  357.7 14.4 %fusion = f32[1792,512]{1,0:T(8,128)S(1)} fusion(f32[1024,512]{1,0:T(8,128)S(1)} %bitcast_subtract_fusion.1, f32[1024,384]{1,0:T(8,128)} %collective-permute-done.7, f32[1024,1024]{1,0:T(8,128)S(1)} %copy-done.6, f32[1024,384]{1,0:T(8,128)} %collective-permute-done.6), kind=kOutput, calls=%fused_computation.13 | convolution fusion | flops 11277959168 | bytes 13107200 | tf_op jit(solution)/shard_map/dot_general | solution.py:81
  372.7 24.0 %fusion.6 = f32[1024,1792]{1,0:T(8,128)S(1)} fusion(f32[224,8,4,128]{3,2,1,0:T(4,128)S(1)} %bitcast.140, f32[1792,512]{1,0:T(8,128)S(1)} %fusion, f32[128,1024]{1,0:T(8,128)S(1)} %fusion.69, f32[128,1024]{1,0:T(8,128)S(1)} %fusion.67, f32[128,1024]{1,0:T(8,128)S(1)} %fusion.65, f32[128,1024]{1,0:T(8,128)S(1)} %fusion.64), kind=kOutput, calls=%fused_computation.23 | convolution fusion | flops 11277697024 | bytes 16777216 | tf_op jit(solution)/shard_map/dot_general | solution.py:93
  396.7 2.9 copy-done.2
  399.7 1.9 fusion.80
  401.6 3.3 collective-permute-start.8
  405.0 2.6 collective-permute-start.9
  408.0 27.8 %collective-permute-done.8 = f32[1024,384]{1,0:T(8,128)S(1)} collective-permute-done((f32[1024,384]{1,0:T(8,128)}, f32[1024,384]{1,0:T(8,128)S(1)}, u32[]{:S(2)}, u32[]{:S(2)}) %collective-permute-start.8) | collective-permute-done | bytes 1572896 | tf_op jit(solution)/shard_map/ppermute | solution.py:23
  435.8 3.2 collective-permute-done.9
  439.0 2.8 slice_select_fusion.1
  444.0 101.9 %all_to_all.65 = f32[32,32,1024]{2,1,0:T(8,128)S(1)} all-to-all(f32[32,32,1024]{2,1,0:T(8,128)S(1)} %maximum_add_fusion), channel_id=1, replica_groups=mesh['member'=32,'region'=8] {'member'}, dimensions={0} | all-to-all | bytes 8388608 | tf_op jit(solution)/shard_map/all_to_all | solution.py:192
  545.8 2.3 copy.95
  (154 shorter events, 36.2 us)
Async XLA Ops:
  0.0 72.2 %copy-start = (f32[32,4096]{1,0:T(8,128)S(1)}, f32[32,4096]{1,0:T(8,128)}, u32[]{:S(2)}) copy-start(f32[32,4096]{1,0:T(8,128)} %param.17) | copy-start | bytes 1572868
  66.5 5.7 %copy-start.23 = (s32[1,2,4]{2,1,0:T(2,128)S(1)}, s32[1,2,4]{2,1,0:T(2,128)}, u32[]{:S(2)}) copy-start(s32[1,2,4]{2,1,0:T(2,128)} %param.22) | copy-start | bytes 100
  66.5 54.2 %all-to-all-start.1 = ((f32[32,16,1024]{2,1,0:T(8,128)}), f32[32,16,1024]{2,1,0:T(8,128)S(1)}, u32[]{:S(2)}, u32[]{:S(2)}) async-start(f32[32,16,1024]{2,1,0:T(8,128)} %get-tuple-element.37), calls=%async_computation.1 | async-start | bytes 4194304 | tf_op jit(solution)/shard_map/all_to_all | solution.py:50
  72.2 8.5 %copy-start.14 = (f32[4096]{0:T(1024)S(1)}, f32[4096]{0:T(1024)}, u32[]{:S(2)}) copy-start(f32[4096]{0:T(1024)} %param.19) | copy-start | bytes 49156
  72.2 3.1 copy-start.21
  72.2 6.7 %copy-start.19 = (pred[4]{0:T(512)(128)(4,1)}, pred[4]{0:T(512)(128)(4,1)S(1)}, u32[]{:S(2)}) copy-start(pred[4]{0:T(512)(128)(4,1)S(1)} %get-tuple-element.55) | copy-start | bytes 16
  72.3 3.1 copy-start.17
  72.3 13.7 %copy-start.13 = (f32[32,32,128]{2,0,1:T(8,128)}, f32[32,32,128]{2,0,1:T(8,128)S(1)}, u32[]{:S(2)}) copy-start(f32[32,32,128]{2,0,1:T(8,128)S(1)} %copy_bitcast_fusion.1) | copy-start | bytes 1572868
  75.3 10.7 %collective-permute-start = (f32[32,4,128]{2,0,1:T(8,128)}, f32[32,4,128]{2,0,1:T(8,128)S(1)}, u32[]{:S(2)}, u32[]{:S(2)}) collective-permute-start(f32[32,4,128]{2,0,1:T(8,128)} %get-tuple-element.62), channel_id=1, source_target_pairs={{7,0},{0,1},{1,2},{2,3},{3,4},{4,5},{5,6},{6,7},{15,8},{8,9},{9,10... | collective-permute-start | bytes 196616 | tf_op jit(solution)/shard_map/ppermute | solution.py:17
  75.3 3.6 copy-start.18
  77.2 8.8 %collective-permute-start.1 = (f32[32,4,128]{2,0,1:T(8,128)}, f32[32,4,128]{2,0,1:T(8,128)S(1)}, u32[]{:S(2)}, u32[]{:S(2)}) collective-permute-start(f32[32,4,128]{2,0,1:T(8,128)} %get-tuple-element.64), channel_id=1, source_target_pairs={{1,0},{2,1},{3,2},{4,3},{5,4},{6,5},{7,6},{0,7},{9,8},{10,9},{11,1... | collective-permute-start | bytes 196616 | tf_op jit(solution)/shard_map/ppermute | solution.py:17
  78.9 10.4 %collective-permute-start.4 = (f32[32,4,128]{2,0,1:T(8,128)}, f32[32,4,128]{2,0,1:T(8,128)S(1)}, u32[]{:S(2)}, u32[]{:S(2)}) collective-permute-start(f32[32,4,128]{2,0,1:T(8,128)} %get-tuple-element.61), channel_id=1, source_target_pairs={{7,0},{0,1},{1,2},{2,3},{3,4},{4,5},{5,6},{6,7},{15,8},{8,9},{9,10... | collective-permute-start | bytes 196616 | tf_op jit(solution)/shard_map/ppermute | solution.py:17
  78.9 10.4 %collective-permute-start.5 = (f32[32,4,128]{2,0,1:T(8,128)}, f32[32,4,128]{2,0,1:T(8,128)S(1)}, u32[]{:S(2)}, u32[]{:S(2)}) collective-permute-start(f32[32,4,128]{2,0,1:T(8,128)} %get-tuple-element.63), channel_id=1, source_target_pairs={{1,0},{2,1},{3,2},{4,3},{5,4},{6,5},{7,6},{0,7},{9,8},{10,9},{11,1... | collective-permute-start | bytes 196616 | tf_op jit(solution)/shard_map/ppermute | solution.py:17
  82.7 48.1 %collective-permute-start.2 = (f32[4,128]{1,0:T(4,128)}, f32[4,128]{1,0:T(4,128)}, u32[]{:S(2)}, u32[]{:S(2)}) collective-permute-start(f32[4,128]{1,0:T(4,128)} %broadcast_select_fusion.3), channel_id=1, source_target_pairs={{7,0},{0,1},{1,2},{2,3},{3,4},{4,5},{5,6},{6,7},{15,8},{8,9},{9,10... | collective-permute-start | bytes 6152 | tf_op jit(solution)/shard_map/ppermute | solution.py:17
  89.4 2.3 copy-start.24
  105.1 23.4 %copy-start.16 = (f32[4,128]{1,0:T(4,128)S(1)}, f32[4,128]{1,0:T(4,128)}, u32[]{:S(2)}) copy-start(f32[4,128]{1,0:T(4,128)} %gather_fusion.5) | copy-start | bytes 6148
  105.1 23.4 %copy-start.20 = (pred[4]{0:T(512)(128)(4,1)S(1)}, pred[4]{0:T(512)(128)(4,1)}, u32[]{:S(2)}) copy-start(pred[4]{0:T(512)(128)(4,1)} %copy-done.19) | copy-start | bytes 16
  105.1 23.5 %copy-start.15 = (s32[1,32,4]{1,2,0:T(4,128)S(1)}, s32[1,32,4]{1,2,0:T(4,128)}, u32[]{:S(2)}) copy-start(s32[1,32,4]{1,2,0:T(4,128)} %param.21) | copy-start | bytes 1540
  105.1 23.7 %copy-start.22 = (s32[1,256,4]{1,2,0:T(4,128)S(1)}, s32[1,256,4]{1,2,0:T(4,128)}, u32[]{:S(2)}) copy-start(s32[1,256,4]{1,2,0:T(4,128)} %param.23) | copy-start | bytes 12292
  120.7 1.3 copy-start.7
  122.0 54.6 %all-to-all-start.2 = ((f32[32,32,512]{2,0,1:T(8,128)}), f32[32,32,512]{2,0,1:T(8,128)S(1)}, u32[]{:S(2)}, u32[]{:S(2)}) async-start(f32[32,32,512]{2,0,1:T(8,128)} %copy.78), calls=%async_computation.2 | async-start | bytes 4194304 | tf_op jit(solution)/shard_map/all_to_all | solution.py:149
  128.6 2.2 collective-permute-start.3
  139.1 4.3 copy-start.9
  143.4 1.6 copy-start.8
  145.3 2.2 copy-start.3
  147.5 2.9 copy-start.5
  150.4 205.4 %collective-permute-start.6 = (f32[1024,384]{1,0:T(8,128)}, f32[1024,384]{1,0:T(8,128)}, u32[]{:S(2)}, u32[]{:S(2)}) collective-permute-start(f32[1024,384]{1,0:T(8,128)} %get-tuple-element.35), channel_id=1, source_target_pairs={{0,8},{8,16},{16,24},{24,32},{32,40},{40,48},{48,56},{56,64},{64,7... | collective-permute-start | bytes 4718600 | tf_op jit(solution)/shard_map/ppermute | solution.py:23
  153.8 202.1 %collective-permute-start.7 = (f32[1024,384]{1,0:T(8,128)}, f32[1024,384]{1,0:T(8,128)}, u32[]{:S(2)}, u32[]{:S(2)}) collective-permute-start(f32[1024,384]{1,0:T(8,128)} %get-tuple-element.36), channel_id=1, source_target_pairs={{8,0},{16,8},{24,16},{32,24},{40,32},{48,40},{56,48},{64,56},{72,6... | collective-permute-start | bytes 4718600 | tf_op jit(solution)/shard_map/ppermute | solution.py:23
  176.6 163.7 %all-to-all-start.3 = ((f32[32,32,512]{2,0,1:T(8,128)}), f32[32,32,512]{2,0,1:T(8,128)}, u32[]{:S(2)}, u32[]{:S(2)}) async-start(f32[32,32,512]{2,0,1:T(8,128)} %copy.84), calls=%async_computation.3 | async-start | bytes 4194304 | tf_op jit(solution)/shard_map/all_to_all | solution.py:150
  193.1 1.0 copy-start.12
  343.4 4.1 copy-start.10
  343.4 4.1 copy-start.11
  355.5 2.2 copy-start.6
  396.7 2.9 copy-start.2
  399.7 7.9 %copy-start.25 = (s32[1,33]{1,0:T(1,128)S(1)}, s32[1,33]{1,0:T(1,128)}, u32[]{:S(2)}) copy-start(s32[1,33]{1,0:T(1,128)} %param.20) | copy-start | bytes 400
  401.6 34.1 %collective-permute-start.8 = (f32[1024,384]{1,0:T(8,128)}, f32[1024,384]{1,0:T(8,128)S(1)}, u32[]{:S(2)}, u32[]{:S(2)}) collective-permute-start(f32[1024,384]{1,0:T(8,128)} %get-tuple-element.33), channel_id=1, source_target_pairs={{0,8},{8,16},{16,24},{24,32},{32,40},{40,48},{48,56},{56,64},{64,7... | collective-permute-start | bytes 4718600 | tf_op jit(solution)/shard_map/ppermute | solution.py:23
  405.0 34.0 %collective-permute-start.9 = (f32[1024,384]{1,0:T(8,128)}, f32[1024,384]{1,0:T(8,128)}, u32[]{:S(2)}, u32[]{:S(2)}) collective-permute-start(f32[1024,384]{1,0:T(8,128)} %get-tuple-element.34), channel_id=1, source_target_pairs={{8,0},{16,8},{24,16},{32,24},{40,32},{48,40},{56,48},{64,56},{72,6... | collective-permute-start | bytes 4718600 | tf_op jit(solution)/shard_map/ppermute | solution.py:23
  439.0 2.8 slice-start
  439.0 4.0 copy-start.4
  545.8 2.3 copy-start.1
where the time goes:
time: 558 us; the launch traced here: 548 us
  blocking collectives  164 us (29%)
  other arithmetic  141 us (25%)
  local copies, waits for them, and re-layouts  75.5 us (14%)
  waiting for transfers between devices  65.8 us (12%)
  matrix products  62.8 us (11%)
  starting transfers between devices  35.9 us (6%)
    all_to_all x1, blocking collectives, body(): lax.all_to_all(states + full_inc, 'member', split_axis=0, concat_axis=1,...  102 us
    another operation x14, other arithmetic, local_solve(): factor = jnp.linalg.cholesky(cov_obs)  81 us
    all_to_all x1, blocking collectives, cut_exchange(): lax.all_to_all(piece, axis, split_axis=0, concat_axis=0, tiled=True)  62.1 us
    another operation x3, other arithmetic, local_solve(): weights = jax.scipy.linalg.cho_solve((factor, True), innovated.T)  41.7 us
    ppermute x4, waiting for transfers between devices, from_behind_2(): return lax.ppermute(block, axis, route)  31 us
    dot_general x1, matrix products, update(): lax.dot_general(weights, kalman_gain, (((0,), (1,)), ((), ())), precision...  24 us
    all_to_all x1, waiting for transfers between devices, body(): lax.all_to_all(send_pred, 'member', split_axis=1, concat_axis=0, tiled=True)  19.2 us
    all_to_all x1, waiting for transfers between devices, cut_exchange(): lax.all_to_all(piece, axis, split_axis=0, concat_axis=0, tiled=True)  15.6 us
  transfers between devices with their start and end apart: 13, of which 4 were waited for; matrix products, arithmetic and copies ran while one was open for 38% of the time, Pallas kernels for 0%

commit v1 on v0

v1 whole, which is shorter than its diff:
```python
import jax
import jax.numpy as jnp
from jax import lax
from jax.experimental import pallas as pl
from jax.experimental.pallas import tpu as pltpu
from jax.sharding import PartitionSpec as P

PIECE = 128
OBS_PER = 4
LOCAL = 512
HALF = 3
ROWS, COLS = 8, 4
BOTH = ("member", "region")

highest = lax.Precision.HIGHEST
f32 = jnp.float32
in_vmem = pl.BlockSpec(memory_space=pltpu.VMEM)
in_smem = pl.BlockSpec(memory_space=pltpu.SMEM)


def dot(a, b, da, db):
    return lax.dot_general(
        a, b, (((da,), (db,)), ((), ())), precision=highest, preferred_element_type=f32
    )


def column_of(z, r, core):
    return ((r if z % 2 == 0 else COLS - 1 - r) + 2 * core) % COLS


def place_on_row(z, y, core):
    r = lax.rem(y + 2 * core, COLS)
    return jnp.where(lax.rem(z, 2) == 0, r, COLS - 1 - r)


def along_snake(x, step):
    regions = lax.axis_size("region")
    total = ROWS * COLS
    route = []
    for g in range(regions):
        spot = [z * COLS + column_of(z, r, g % 2) for z in range(ROWS) for r in range(COLS)]
        for p in range(total):
            if 0 <= p + step < total:
                route.append((spot[p] * regions + g, spot[p + step] * regions + g))
    return lax.ppermute(x, BOTH, route)


def exchange(x):
    return lax.all_to_all(x, "member", split_axis=0, concat_axis=0, tiled=True)


def states_kernel(core_ref, x_ref, rim_ref, mid_ref):
    z = pl.program_id(0)
    for y in range(COLS):
        base = place_on_row(z, y, core_ref[0]) * 1024
        rim_ref[y, :, :384] = x_ref[:, pl.ds(pl.multiple_of(base, 128), 384)]
        mid_ref[y] = x_ref[:, pl.ds(pl.multiple_of(base + 384, 128), 256)]
        rim_ref[y, :, 384:] = x_ref[:, pl.ds(pl.multiple_of(base + 640, 128), 384)]


def lay_states(core, x):
    members = x.shape[0]
    widths = (768, 256)
    return pl.pallas_call(
        states_kernel,
        grid=(ROWS,),
        in_specs=[in_smem, pl.BlockSpec((members, 4096), lambda z: (0, z))],
        out_specs=[pl.BlockSpec((COLS, members, w), lambda z: (z, 0, 0)) for w in widths],
        out_shape=[jax.ShapeDtypeStruct((ROWS * COLS, members, w), f32) for w in widths],
        compiler_params=pltpu.CompilerParams(vmem_limit_bytes=16 * 2**20),
        cost_estimate=pl.CostEstimate(flops=0, bytes_accessed=2**23, transcendentals=0),
    )(core, x)


def halo_kernel(ids_ref, pred_ref, innov_ref, var_ref, before_ref, after_ref):
    members = pred_ref.shape[0]
    for j, out_ref in enumerate((before_ref, after_ref)):
        for k in range(4):
            at = pl.ds(pl.multiple_of(ids_ref[j, k] * PIECE, PIECE), PIECE)
            to = slice(k * PIECE, (k + 1) * PIECE)
            out_ref[:members, to] = pred_ref[:, at]
            out_ref[members : 2 * members, to] = innov_ref[:, at]
            out_ref[2 * members :, to] = jnp.broadcast_to(var_ref[:, at], (8, PIECE))


def lay_halo(ids, pred, innov, var):
    rows = 2 * pred.shape[0] + 8
    return pl.pallas_call(
        halo_kernel,
        in_specs=[in_smem, in_vmem, in_vmem, in_vmem],
        out_specs=[in_vmem, in_vmem],
        out_shape=[jax.ShapeDtypeStruct((rows, LOCAL), f32)] * 2,
        compiler_params=pltpu.CompilerParams(vmem_limit_bytes=8 * 2**20),
        cost_estimate=pl.CostEstimate(flops=0, bytes_accessed=2**20, transcendentals=0),
    )(ids, pred, innov, var)


def obs_kernel(
    place_ref, lists_ref, pred_ref, innov_ref, var_ref, before_ref, after_ref,
    pred_out, innov_out, var_out, pred_ext, innov_ext, var_ext,
):
    members, own = pred_ref.shape
    for ext, ref, lo, hi in (
        (pred_ext, pred_ref, 0, members),
        (innov_ext, innov_ref, members, 2 * members),
    ):
        ext[:, :own] = ref[...]
        ext[:, own : own + LOCAL] = before_ref[lo:hi, :]
        ext[:, own + LOCAL :] = after_ref[lo:hi, :]
    var_ext[:, :own] = jnp.broadcast_to(var_ref[...], (8, own))
    var_ext[:, own : own + LOCAL] = before_ref[2 * members :, :]
    var_ext[:, own + LOCAL :] = after_ref[2 * members :, :]
    core, mine = place_ref[0], place_ref[1]

    def one(i, carry):
        z, y = i // COLS, lax.rem(i, COLS)
        patch = z * COLS + place_on_row(z, y, core)
        for k in range(OBS_PER):
            at = pl.ds(pl.multiple_of(lists_ref[patch, k] * PIECE, PIECE), PIECE)
            to = slice(k * PIECE, (k + 1) * PIECE)
            pred_out[i, :, to] = pred_ext[:, at]
            innov_out[i, :, to] = innov_ext[:, at]
        return carry

    lax.fori_loop(0, ROWS * COLS, one, 0)
    for k in range(OBS_PER):
        at = pl.ds(pl.multiple_of(lists_ref[mine, k] * PIECE, PIECE), PIECE)
        var_out[:, k * PIECE : (k + 1) * PIECE] = var_ext[:, at]


def lay_obs(place, lists, pred, innov, var, before, after):
    members, own = pred.shape
    sent = jax.ShapeDtypeStruct((ROWS * COLS, members, LOCAL), f32)
    return pl.pallas_call(
        obs_kernel,
        in_specs=[in_smem, in_smem] + [in_vmem] * 5,
        out_specs=[in_vmem] * 3,
        out_shape=[sent, sent, jax.ShapeDtypeStruct((8, LOCAL), f32)],
        scratch_shapes=[
            pltpu.VMEM((members, own + 2 * LOCAL), f32),
            pltpu.VMEM((members, own + 2 * LOCAL), f32),
            pltpu.VMEM((8, own + 2 * LOCAL), f32),
        ],
        compiler_params=pltpu.CompilerParams(vmem_limit_bytes=24 * 2**20),
        cost_estimate=pl.CostEstimate(flops=0, bytes_accessed=6 * 2**20, transcendentals=0),
    )(place, lists, pred, innov, var, before, after)


def finish_kernel(core_ref, x_ref, mid_ref, rim_ref, out_ref):
    z = pl.program_id(0)
    for y in range(COLS):
        base = place_on_row(z, y, core_ref[0]) * 1024
        for lo, width, ref, at in ((0, 384, rim_ref, 0), (384, 256, mid_ref, 0), (640, 384, rim_ref, 384)):
            to = pl.ds(pl.multiple_of(base + lo, 128), width)
            out_ref[:, to] = x_ref[:, to] + ref[y, :, at : at + width]


def finish(core, x, mid, rim):
    members = x.shape[0]
    return pl.pallas_call(
        finish_kernel,
        grid=(ROWS,),
        in_specs=[
            in_smem,
            pl.BlockSpec((members, 4096), lambda z: (0, z)),
            pl.BlockSpec((COLS, members, 256), lambda z: (z, 0, 0)),
            pl.BlockSpec((COLS, members, 768), lambda z: (z, 0, 0)),
        ],
        out_specs=pl.BlockSpec((members, 4096), lambda z: (0, z)),
        out_shape=jax.ShapeDtypeStruct(x.shape, f32),
        compiler_params=pltpu.CompilerParams(vmem_limit_bytes=16 * 2**20),
        cost_estimate=pl.CostEstimate(flops=2**20, bytes_accessed=3 * 2**22, transcendentals=0),
    )(core, x, mid, rim)


def factor_block(a_ref, m_ref):
    n = PIECE
    row = lax.broadcasted_iota(jnp.int32, (8, n), 0)
    for lo in range(0, n, 8):
        p = a_ref[lo : lo + 8, :]
        q = m_ref[lo : lo + 8, :]
        b = [jnp.broadcast_to(p[:, lo + i : lo + i + 1], (8, n)) for i in range(8)]
        d = jnp.ones((8, n), f32)
        for i in range(8):
            pivot = jnp.broadcast_to(b[i][i : i + 1, :], (8, n))
            d = jnp.where(row == i, pivot, d)
            if i < 7:
                f = jnp.where(row > i, b[i] / pivot, 0.0)
                for j in range(i + 1, 8):
                    b[j] = b[j] - f * jnp.broadcast_to(b[j][i : i + 1, :], (8, n))
                p = p - f * jnp.broadcast_to(p[i : i + 1, :], (8, n))
                q = q - f * jnp.broadcast_to(q[i : i + 1, :], (8, n))
        s = lax.rsqrt(d)
        u = p * s
        v = q * s
        m_ref[lo : lo + 8, :] = v
        if lo + 8 < n:
            step = dot(u.T, jnp.concatenate([u, v], axis=1), 1, 0)
            a_ref[lo + 8 :, :] = a_ref[lo + 8 :, :] - step[lo + 8 :, :n]
            m_ref[lo + 8 :, :] = m_ref[lo + 8 :, :] - step[lo + 8 :, n:]


def factor_kernel(c_ref, t_ref, a_ref, d_ref, m_ref):
    n = PIECE
    a_ref[...] = c_ref[...]
    t_ref[...] = jnp.zeros((LOCAL, LOCAL), f32)
    eye = lax.broadcasted_iota(jnp.int32, (n, n), 0) == lax.broadcasted_iota(jnp.int32, (n, n), 1)
    for lo in range(0, LOCAL, n):
        hi = lo + n
        d_ref[...] = a_ref[lo:hi, lo:hi]
        m_ref[...] = eye.astype(f32)
        factor_block(d_ref, m_ref)
        m = m_ref[...]
        if lo:
            t_ref[lo:hi, :lo] = dot(m, t_ref[lo:hi, :lo], 1, 0)
        t_ref[lo:hi, lo:hi] = m
        if hi < LOCAL:
            u = dot(m, a_ref[lo:hi, hi:], 1, 0)
            a_ref[hi:, hi:] = a_ref[hi:, hi:] - dot(u, u, 0, 0)
            t_ref[hi:, :hi] = t_ref[hi:, :hi] - dot(u, t_ref[lo:hi, :hi], 0, 0)


def inverse_factor(cov):
    return pl.pallas_call(
        factor_kernel,
        in_specs=[in_vmem],
        out_specs=in_vmem,
        out_shape=jax.ShapeDtypeStruct((LOCAL, LOCAL), f32),
        scratch_shapes=[
            pltpu.VMEM((LOCAL, LOCAL), f32),
            pltpu.VMEM((PIECE, PIECE), f32),
            pltpu.VMEM((PIECE, PIECE), f32),
        ],
        compiler_params=pltpu.CompilerParams(vmem_limit_bytes=16 * 2**20),
        cost_estimate=pl.CostEstimate(flops=36 * 10**9, bytes_accessed=2**21, transcendentals=0),
    )(cov)


def in_order(*arrays):
    return lax.optimization_barrier(arrays)


def body(
    background_realizations,
    realization_expected_data,
    departure_values,
    instrument_dispersion,
    window_piece_offsets,
    window_data_pieces,
    neighbor_piece_ids,
    coupling_indicator,
):
    own_index = lax.axis_index("member")
    region = lax.axis_index("region")
    regions = lax.axis_size("region")
    members = lax.axis_size("member") * background_realizations.shape[0]
    core = lax.rem(region, 2)
    z, y = own_index // COLS, lax.rem(own_index, COLS)
    mine = z * COLS + place_on_row(z, y, core)
    core_word = core.reshape(1)

    rim_s, mid_s = lay_states(core_word, background_realizations)
    rim = exchange(rim_s)

    var = instrument_dispersion.reshape(1, -1)
    to_next, to_last = lay_halo(
        neighbor_piece_ids[0], realization_expected_data, departure_values, var
    )
    before = lax.ppermute(to_next, "region", [(i, (i + 1) % regions) for i in range(regions)])
    behind = lax.ppermute(to_last, "region", [(i, (i - 1) % regions) for i in range(regions)])
    pred_s, innov_s, var_rows = lay_obs(
        jnp.stack([core, mine]),
        window_data_pieces[0],
        realization_expected_data,
        departure_values,
        var,
        before,
        behind,
    )

    def whole(x):
        return x.reshape(members, x.shape[2])

    def in_parts(x):
        return x.reshape(lax.axis_size("member"), -1, x.shape[1])

    cover = jnp.pad(coupling_indicator[0].astype(f32), ((HALF, HALF), (0, 0)))
    cover = lax.dynamic_slice_in_dim(cover, 8 * mine, 14, 0)
    cover = jnp.broadcast_to(cover[:, :, None], (14, OBS_PER, PIECE)).reshape(14, LOCAL)
    starts = lax.dynamic_slice_in_dim(window_piece_offsets[0], mine, 2, 0) - 8 * mine
    block = lax.broadcasted_iota(jnp.int32, (1, 384), 1) // PIECE

    rim = whole(rim)
    head, tail = rim[:, :384], rim[:, 384:]
    rim, pred_s = in_order(rim, pred_s)
    pred = exchange(pred_s)
    beyond = along_snake(head, -1)
    ahead = along_snake(tail, 1)

    pred, innov_s = in_order(pred, innov_s)
    innov = exchange(innov_s)
    pred = whole(pred)
    perturbed = pred - jnp.mean(pred, axis=0, keepdims=True)
    cov = dot(perturbed, perturbed, 0, 0) / (members - 1.0)
    cov = cov + jnp.eye(LOCAL, dtype=f32) * var_rows[:1]
    root = inverse_factor(cov)

    def gain(x, lo):
        count = x.shape[1] // PIECE
        centred = x - jnp.mean(x, axis=0, keepdims=True)
        g = dot(centred, perturbed, 0, 0) / (members - 1.0)
        g = g.reshape(count, PIECE, LOCAL) * cover[lo : lo + count, None, :]
        return g.reshape(count * PIECE, LOCAL)

    root, beyond, ahead = in_order(root, beyond, ahead)
    beyond_gain = gain(beyond, 11)
    ahead_gain = gain(ahead, 0)

    innov, root, mid_s, beyond_gain, ahead_gain = in_order(innov, root, mid_s, beyond_gain, ahead_gain)
    mid = exchange(mid_s)
    weights = dot(root, dot(root, whole(innov), 1, 1), 0, 0)
    beyond_inc = dot(weights, beyond_gain, 0, 1)
    ahead_inc = dot(weights, ahead_gain, 0, 1)
    head_back = along_snake(beyond_inc, 1)
    tail_back = along_snake(ahead_inc, -1)
    mid, beyond_inc, ahead_inc = in_order(mid, beyond_inc, ahead_inc)
    mid_inc = dot(weights, gain(whole(mid), 6), 0, 1)
    mid_out = exchange(in_parts(mid_inc))
    mid_inc, late_weights, head, tail = in_order(mid_inc, weights, head, tail)
    head_own = dot(late_weights, gain(head, 3), 0, 1)
    tail_own = dot(late_weights, gain(tail, 8), 0, 1)
    head_own, tail_own, head_back, tail_back = in_order(head_own, tail_own, head_back, tail_back)
    head_inc = jnp.where(block < starts[0], head_back, head_own)
    tail_inc = jnp.where(block + 5 >= starts[1], tail_back, tail_own)
    rim_inc = jnp.concatenate([head_inc, tail_inc], axis=1)
    mid_out, rim_inc = in_order(mid_out, rim_inc)
    rim_out = exchange(in_parts(rim_inc))
    return finish(core_word, background_realizations, mid_out, rim_out)


def solution(mesh):
    return jax.shard_map(
        body,
        mesh=mesh,
        in_specs=(
            P("member", "region"),
            P("member", "region"),
            P("member", "region"),
            P("region"),
            P("region", None),
            P("region", None, None),
            P("region", None, None),
            P("region", None, None),
        ),
        out_specs=P("member", "region"),
        check_vma=False,
    )
```

time: 558 us -> 390 us (0.70); the launches traced: 548 us -> 386 us
  other arithmetic: 141 us -> 13.7 us
  blocking collectives: 164 us -> 79.5 us
  local copies, waits for them, and re-layouts: 75.5 us -> 8.2 us
  Pallas kernels: 0 us -> 49.6 us
  waiting for transfers between devices: 65.8 us -> 105 us
  starting transfers between devices: 35.9 us -> 58.5 us
  matrix products: 62.8 us -> 70.5 us
    another operation x17 -> x1, other arithmetic: 123 us -> 0.07 us  [body(): jnp.stack([core, mine])]
    all_to_all x2 -> x1, blocking collectives: 164 us -> 79.5 us  [exchange(): return lax.all_to_all(x, 'member', split_axis=0, concat_axis=0, tiled=True)]
    all_to_all x3 -> x5, waiting for transfers between devices: 34.8 us -> 103 us  [exchange(): return lax.all_to_all(x, 'member', split_axis=0, concat_axis=0, tiled=True)]
    pallas_call x0 -> x5, Pallas kernels: none -> 49.6 us  [the longest x1 37.4 us: inverse_factor(): pl.pallas_call(factor_kernel, in_specs=[in_vmem], out_specs=in_vmem, out_...]
    ppermute x10 -> x6, waiting for transfers between devices: 31 us -> 2.67 us  [the longest x1 2.66 us: body(): lax.ppermute(to_next, 'region', [(i, (i + 1) % regions) for i in range(re...]
    dot_general x3 -> x13, matrix products: 43.1 us -> 70.5 us  [dot(): lax.dot_general(a, b, (((da,), (db,)), ((), ())), precision=highest, pref...]
    all_to_all x3 -> x5, starting transfers between devices: 19.6 us -> 44 us  [exchange(): return lax.all_to_all(x, 'member', split_axis=0, concat_axis=0, tiled=True)]
    another operation x20 -> x0, matrix products: 19.8 us -> none  [the longest x14 12 us: local_solve(): weights = jax.scipy.linalg.cho_solve((factor, True), innovated.T)]
  transfers between devices with their start and end apart: 13 -> 11, of which waited for: 4 -> 3; matrix products, arithmetic and copies ran while one was open for 38% -> 23% of each run, Pallas kernels for 0% -> 11%
where the time goes in v1:
time: 390 us; the launch traced here: 386 us
  waiting for transfers between devices  105 us (27%)
  blocking collectives  79.5 us (20%)
  matrix products  70.5 us (18%)
  starting transfers between devices  58.5 us (15%)
  Pallas kernels  49.6 us (13%)
  other arithmetic  13.7 us (4%)
  local copies, waits for them, and re-layouts  8.2 us (2%)
    all_to_all x5, waiting for transfers between devices, exchange(): return lax.all_to_all(x, 'member', split_axis=0, concat_axis=0, tiled=True)  103 us
    all_to_all x1, blocking collectives, exchange(): return lax.all_to_all(x, 'member', split_axis=0, concat_axis=0, tiled=True)  79.5 us
    dot_general x13, matrix products, dot(): lax.dot_general(a, b, (((da,), (db,)), ((), ())), precision=highest, pref...  70.5 us
    all_to_all x5, starting transfers between devices, exchange(): return lax.all_to_all(x, 'member', split_axis=0, concat_axis=0, tiled=True)  44 us
    pallas_call x1, Pallas kernels, inverse_factor(): pl.pallas_call(factor_kernel, in_specs=[in_vmem], out_specs=in_vmem, out_...  37.4 us
    ppermute x4, starting transfers between devices, along_snake(): return lax.ppermute(x, BOTH, route)  12.8 us
  transfers between devices with their start and end apart: 11, of which 3 were waited for; matrix products, arithmetic and copies ran while one was open for 23% of the time, Pallas kernels for 11%

profile of v1, /device:TPU:12, one launch (start us, length us, event | category | flops | bytes accessed | tf_op | source)
XLA Modules:
  0.0 385.9 jit_solution(17269897903014037294)
XLA Ops:
  0.0 2.2 copy-done
  2.2 3.7 shard_map.82
  5.9 11.9 %all-to-all-start = ((f32[32,32,768]{2,1,0:T(8,128)}), f32[32,32,768]{2,1,0:T(8,128)}, u32[]{:S(2)}, u32[]{:S(2)}) async-start(f32[32,32,768]{2,1,0:T(8,128)} %get-tuple-element.33), calls=%async_computation | async-start | bytes 6291456 | tf_op jit(solution)/shard_map/all_to_all | solution.py:49
  17.9 0.6 shard_map.83
  18.5 1.7 collective-permute-start.1
  20.2 0.1 copy.9.lists_ref
  20.3 0.1 pad_add_fusion.place_ref
  20.4 2.7 collective-permute-done.before_ref
  23.0 4.0 %shard_map.84 = (f32[32,32,512]{2,1,0:T(8,128)}, f32[32,32,512]{2,1,0:T(8,128)}, f32[8,512]{1,0:T(8,128)S(1)}) custom-call(s32[2]{0:T(128)S(1)} %pad_add_fusion.place_ref, s32[32,4]{1,0:T(8,128)S(1)} %copy.9.lists_ref, f32[32,4096]{1,0:T(8,128)S(1)} %copy-done.2, f32[32,4096]{1,0:T(8,128)S(1)} %copy-done.3, f32[1,4096]{1,0:T(1,128)S(1)} %bitcast.77, ...), custom_call_target="tpu_custom_call" | custom-call | bytes 6291456 | tf_op jit(solution)/shard_map/pallas_call | solution.py:134
  27.1 62.1 %all-to-all-done = f32[32,32,768]{2,1,0:T(8,128)} async-done(((f32[32,32,768]{2,1,0:T(8,128)}), f32[32,32,768]{2,1,0:T(8,128)}, u32[]{:S(2)}, u32[]{:S(2)}) %all-to-all-start) | async-done | bytes 3145760 | tf_op jit(solution)/shard_map/all_to_all | solution.py:49
  89.1 7.5 %all-to-all-start.1 = ((f32[32,32,512]{2,1,0:T(8,128)}), f32[32,32,512]{2,1,0:T(8,128)S(1)}, u32[]{:S(2)}, u32[]{:S(2)}) async-start(f32[32,32,512]{2,1,0:T(8,128)} %get-tuple-element.37), calls=%async_computation.1 | async-start | bytes 4194304 | tf_op jit(solution)/shard_map/all_to_all | solution.py:49
  96.6 0.1 pad_dynamic-slice_fusion
  96.7 0.1 slice.47
  96.9 0.1 copy.10
  97.0 0.1 broadcast_bitcast_fusion.3
  97.0 0.1 copy.11
  97.1 0.1 broadcast_bitcast_fusion.2
  97.2 0.1 copy.12
  97.3 0.1 broadcast_bitcast_fusion.4
  97.4 0.1 copy.13
  97.5 0.1 broadcast_bitcast_fusion.1
  97.6 0.1 copy.14
  97.6 3.8 fusion.68
  101.5 2.1 collective-permute-start.2
  103.6 3.7 collective-permute-start.3
  107.3 40.5 %all-to-all-done.1 = f32[32,32,512]{2,1,0:T(8,128)S(1)} async-done(((f32[32,32,512]{2,1,0:T(8,128)}), f32[32,32,512]{2,1,0:T(8,128)S(1)}, u32[]{:S(2)}, u32[]{:S(2)}) %all-to-all-start.1) | async-done | bytes 2097184 | tf_op jit(solution)/shard_map/all_to_all | solution.py:49
  147.8 5.9 %all-to-all-start.2 = ((f32[32,32,512]{2,1,0:T(8,128)}), f32[32,32,512]{2,1,0:T(8,128)}, u32[]{:S(2)}, u32[]{:S(2)}) async-start(f32[32,32,512]{2,1,0:T(8,128)} %get-tuple-element.39), calls=%async_computation.2 | async-start | bytes 4194304 | tf_op jit(solution)/shard_map/all_to_all | solution.py:49
  153.7 0.2 reduce_sum.54
  153.9 3.6 fusion.18.c_ref
  157.5 37.4 %shard_map.85 = f32[512,512]{1,0:T(8,128)S(1)} custom-call(f32[512,512]{1,0:T(8,128)S(1)} %fusion.18.c_ref), custom_call_target="tpu_custom_call" | custom-call | flops 35999997952 | bytes 2097152 | tf_op jit(solution)/shard_map/pallas_call | solution.py:224
  194.9 1.6 reduce_sum.55
  196.5 1.6 reduce_sum.56
  198.1 0.3 bitcast_subtract_fusion
  198.3 0.1 mul.92
  198.4 6.0 %fusion.24 = f32[384,512]{1,0:T(8,128)} fusion(f32[384,512]{1,0:T(8,128)S(1)} %bitcast.82, f32[1024,512]{1,0:T(8,128)S(1)} %bitcast_subtract_fusion, f32[1024,384]{1,0:T(8,128)} %collective-permute-done.2, f32[384]{0:T(512)S(1)} %broadcast_multiply_fusion.3), kind=kOutput, calls=%fused_computation.18 | convolution fusion | flops 2416705536 | bytes 5244416 | tf_op jit(solution)/shard_map/dot_general | solution.py:22
  204.4 0.1 mul.96
  204.5 5.1 %fusion.30 = f32[384,512]{1,0:T(8,128)} fusion(f32[384,512]{1,0:T(8,128)S(1)} %bitcast.83, f32[1024,512]{1,0:T(8,128)S(1)} %bitcast_subtract_fusion, f32[1024,384]{1,0:T(8,128)} %collective-permute-done.3, f32[384]{0:T(512)S(1)} %broadcast_multiply_fusion.2), kind=kOutput, calls=%fused_computation.20 | convolution fusion | flops 2416705536 | bytes 5244416 | tf_op jit(solution)/shard_map/dot_general | solution.py:22
  209.6 10.0 %all-to-all-start.3 = ((f32[32,32,256]{2,1,0:T(8,128)}), f32[32,32,256]{2,1,0:T(8,128)}, u32[]{:S(2)}, u32[]{:S(2)}) async-start(f32[32,32,256]{2,1,0:T(8,128)} %get-tuple-element.48), calls=%async_computation.3 | async-start | bytes 2097152 | tf_op jit(solution)/shard_map/all_to_all | solution.py:49
  219.7 0.1 dynamic-slice_subtract_fusion
  219.8 0.6 fusion.70
  220.3 0.6 fusion.66
  220.9 0.7 fusion.65
  221.6 5.2 %fusion.71 = f32[512,1024]{1,0:T(8,128)S(1)} fusion(f32[512,512]{1,0:T(8,128)S(1)} %shard_map.85, f32[1024,512]{1,0:T(8,128)} %bitcast.12), kind=kOutput, calls=%fused_computation.72 | convolution fusion | flops 3221225472 | bytes 5242880 | tf_op jit(solution)/shard_map/dot_general | solution.py:22
  226.8 3.5 fusion.72
  230.4 8.2 %fusion.73 = f32[1024,384]{1,0:T(8,128)} fusion(f32[512,1024]{1,0:T(8,128)S(1)} %fusion.72, f32[384,512]{1,0:T(8,128)S(1)} %copy-done.9), kind=kOutput, calls=%fused_computation.74 | convolution fusion | flops 2415919104 | bytes 4456448 | tf_op jit(solution)/shard_map/dot_general | solution.py:22
  238.6 3.4 collective-permute-start.4
  242.0 7.9 %fusion.74 = f32[1024,384]{1,0:T(8,128)} fusion(f32[512,1024]{1,0:T(8,128)S(1)} %fusion.72, f32[384,512]{1,0:T(8,128)S(1)} %copy-done.10), kind=kOutput, calls=%fused_computation.75 | convolution fusion | flops 2415919104 | bytes 4456448 | tf_op jit(solution)/shard_map/dot_general | solution.py:22
  249.9 3.6 collective-permute-start.5
  253.5 1.4 reduce_sum.57
  254.9 4.0 %fusion.51 = f32[256,512]{1,0:T(8,128)S(1)} fusion(f32[256,512]{1,0:T(8,128)S(1)} %bitcast.85, f32[32,32,512]{2,1,0:T(8,128)} %copy-done.8, f32[32,32,256]{2,1,0:T(8,128)} %all-to-all-done.3, f32[512]{0:T(512)S(1)} %broadcast_multiply_fusion.4, f32[256]{0:T(256)S(1)} %broadcast_multiply_fusion.5), kind=kOutput, calls=%fused_computation.27 | convolution fusion | flops 1611661312 | bytes 4197376 | tf_op jit(solution)/shard_map/dot_general | solution.py:22
  258.9 4.4 %fusion.75 = f32[1024,256]{1,0:T(8,128)} fusion(f32[512,1024]{1,0:T(8,128)S(1)} %fusion.72, f32[256,512]{1,0:T(8,128)S(1)} %fusion.51), kind=kOutput, calls=%fused_computation.76 | convolution fusion | flops 1610612736 | bytes 3670016 | tf_op jit(solution)/shard_map/dot_general | solution.py:22
  263.3 8.8 %all-to-all-start.4 = ((f32[32,32,256]{2,1,0:T(8,128)}), f32[32,32,256]{2,1,0:T(8,128)S(1)}, u32[]{:S(2)}, u32[]{:S(2)}) async-start(f32[32,32,256]{2,1,0:T(8,128)} %bitcast.80), calls=%async_computation.4 | async-start | bytes 2097152 | tf_op jit(solution)/shard_map/all_to_all | solution.py:49
  272.2 1.6 reduce_sum.58
  273.7 1.6 reduce_sum.59
  275.3 0.1 mul.104
  275.4 4.8 %fusion.36 = f32[384,512]{1,0:T(8,128)S(1)} fusion(f32[384,512]{1,0:T(8,128)S(1)} %bitcast.84, f32[1024,512]{1,0:T(8,128)} %copy-done.6, f32[1024,384]{1,0:T(8,128)} %get-tuple-element.53, f32[384]{0:T(512)S(1)} %broadcast_multiply_fusion.1), kind=kOutput, calls=%fused_computation.22 | convolution fusion | flops 2416705536 | bytes 5244416 | tf_op jit(solution)/shard_map/dot_general | solution.py:22
  280.3 6.7 %fusion.76 = f32[1024,384]{1,0:T(8,128)S(1)} fusion(f32[512,1024]{1,0:T(8,128)S(1)} %fusion.72, f32[384,512]{1,0:T(8,128)S(1)} %fusion.36), kind=kOutput, calls=%fused_computation.77 | convolution fusion | flops 2415919104 | bytes 4456448 | tf_op jit(solution)/shard_map/dot_general | solution.py:22
  286.9 0.1 mul.108
  287.0 4.4 %fusion.42 = f32[384,512]{1,0:T(8,128)S(1)} fusion(f32[384,512]{1,0:T(8,128)S(1)} %bitcast.81, f32[1024,512]{1,0:T(8,128)S(1)} %copy-done.7, f32[1024,384]{1,0:T(8,128)} %get-tuple-element.54, f32[384]{0:T(512)S(1)} %broadcast_multiply_fusion), kind=kOutput, calls=%fused_computation.24 | convolution fusion | flops 2416705536 | bytes 5244416 | tf_op jit(solution)/shard_map/dot_general | solution.py:22
  291.5 6.7 %fusion.77 = f32[1024,384]{1,0:T(8,128)S(1)} fusion(f32[512,1024]{1,0:T(8,128)S(1)} %fusion.72, f32[384,512]{1,0:T(8,128)S(1)} %fusion.42), kind=kOutput, calls=%fused_computation.78 | convolution fusion | flops 2415919104 | bytes 4456448 | tf_op jit(solution)/shard_map/dot_general | solution.py:22
  298.2 2.2 broadcast_select_fusion
  300.4 1.9 pad_maximum_fusion
  302.3 79.5 %all_to_all.30.rim_ref = f32[32,32,768]{2,1,0:T(8,128)S(1)} all-to-all(f32[32,32,768]{2,1,0:T(8,128)} %bitcast.79), channel_id=1, replica_groups=mesh['member'=32,'region'=8] {'member'}, dimensions={0} | all-to-all | bytes 6291456 | tf_op jit(solution)/shard_map/all_to_all | solution.py:49
  381.8 3.9 %shard_map.86 = f32[32,32768]{1,0:T(8,128)} custom-call(s32[1]{0:T(128)} %bitcast.core_ref, f32[32,32768]{1,0:T(8,128)S(1)} %copy-done.1, f32[32,32,256]{2,1,0:T(8,128)S(1)} %all-to-all-done.4.mid_ref, f32[32,32,768]{2,1,0:T(8,128)S(1)} %all_to_all.30.rim_ref), custom_call_target="tpu_custom_call" | custom-call | flops 1048576 | bytes 12582912 | tf_op jit(solution)/shard_map/pallas_call | solution.py:160
  (52 shorter events, 0.4 us)
Async XLA Ops:
  0.0 2.2 copy-start
  5.9 11.9 %copy-start.2 = (f32[32,4096]{1,0:T(8,128)S(1)}, f32[32,4096]{1,0:T(8,128)}, u32[]{:S(2)}) copy-start(f32[32,4096]{1,0:T(8,128)} %pred_ref.3) | copy-start | bytes 1572868
  5.9 11.9 %copy-start.3 = (f32[32,4096]{1,0:T(8,128)S(1)}, f32[32,4096]{1,0:T(8,128)}, u32[]{:S(2)}) copy-start(f32[32,4096]{1,0:T(8,128)} %innov_ref.3) | copy-start | bytes 1572868
  5.9 12.0 %copy-start.4 = (f32[4096]{0:T(1024)S(1)}, f32[4096]{0:T(1024)}, u32[]{:S(2)}) copy-start(f32[4096]{0:T(1024)} %param.11) | copy-start | bytes 49156
  5.9 12.0 %copy-start.5 = (s32[1,2,4]{2,1,0:T(2,128)S(1)}, s32[1,2,4]{2,1,0:T(2,128)}, u32[]{:S(2)}) copy-start(s32[1,2,4]{2,1,0:T(2,128)} %param.14) | copy-start | bytes 100
  5.9 14.3 %copy-start.12 = (s32[1,32,4]{1,2,0:T(4,128)S(1)}, s32[1,32,4]{1,2,0:T(4,128)}, u32[]{:S(2)}) copy-start(s32[1,32,4]{1,2,0:T(4,128)} %param.13) | copy-start | bytes 1540
  5.9 83.2 %all-to-all-start = ((f32[32,32,768]{2,1,0:T(8,128)}), f32[32,32,768]{2,1,0:T(8,128)}, u32[]{:S(2)}, u32[]{:S(2)}) async-start(f32[32,32,768]{2,1,0:T(8,128)} %get-tuple-element.33), calls=%async_computation | async-start | bytes 6291456 | tf_op jit(solution)/shard_map/all_to_all | solution.py:49
  18.5 4.6 %collective-permute-start = (f32[72,512]{1,0:T(8,128)S(1)}, f32[72,512]{1,0:T(8,128)S(1)}, u32[]{:S(2)}, u32[]{:S(2)}) collective-permute-start(f32[72,512]{1,0:T(8,128)S(1)} %get-tuple-element.34), channel_id=1, source_target_pairs={{0,1},{1,2},{2,3},{3,4},{4,5},{5,6},{6,7},{7,0},{8,9},{9,10},{10,1... | collective-permute-start | bytes 442376 | tf_op jit(solution)/shard_map/ppermute | solution.py:269
  18.5 4.6 %collective-permute-start.1 = (f32[72,512]{1,0:T(8,128)S(1)}, f32[72,512]{1,0:T(8,128)S(1)}, u32[]{:S(2)}, u32[]{:S(2)}) collective-permute-start(f32[72,512]{1,0:T(8,128)S(1)} %get-tuple-element.35), channel_id=1, source_target_pairs={{0,7},{1,0},{2,1},{3,2},{4,3},{5,4},{6,5},{7,6},{8,15},{9,8},{10,9... | collective-permute-start | bytes 442376 | tf_op jit(solution)/shard_map/ppermute | solution.py:270
  89.1 7.5 %copy-start.11 = (s32[1,256,4]{1,2,0:T(4,128)S(1)}, s32[1,256,4]{1,2,0:T(4,128)}, u32[]{:S(2)}) copy-start(s32[1,256,4]{1,2,0:T(4,128)} %param.15) | copy-start | bytes 12292
  89.1 58.7 %all-to-all-start.1 = ((f32[32,32,512]{2,1,0:T(8,128)}), f32[32,32,512]{2,1,0:T(8,128)S(1)}, u32[]{:S(2)}, u32[]{:S(2)}) async-start(f32[32,32,512]{2,1,0:T(8,128)} %get-tuple-element.37), calls=%async_computation.1 | async-start | bytes 4194304 | tf_op jit(solution)/shard_map/all_to_all | solution.py:49
  101.5 93.4 %collective-permute-start.2 = (f32[1024,384]{1,0:T(8,128)}, f32[1024,384]{1,0:T(8,128)}, u32[]{:S(2)}, u32[]{:S(2)}) collective-permute-start(f32[1024,384]{1,0:T(8,128)} %get-tuple-element.53), channel_id=1, source_target_pairs={{8,0},{16,8},{24,16},{56,24},{48,56},{40,48},{32,40},{64,32},{72,6... | collective-permute-start | bytes 4718600 | tf_op jit(solution)/shard_map/ppermute | solution.py:45
  103.6 91.3 %collective-permute-start.3 = (f32[1024,384]{1,0:T(8,128)}, f32[1024,384]{1,0:T(8,128)}, u32[]{:S(2)}, u32[]{:S(2)}) collective-permute-start(f32[1024,384]{1,0:T(8,128)} %get-tuple-element.54), channel_id=1, source_target_pairs={{0,8},{8,16},{16,24},{24,56},{56,48},{48,40},{40,32},{32,64},{64,7... | collective-permute-start | bytes 4718600 | tf_op jit(solution)/shard_map/ppermute | solution.py:45
  147.8 50.2 %copy-start.8 = (f32[32,32,512]{2,1,0:T(8,128)}, f32[32,32,512]{2,1,0:T(8,128)S(1)}, u32[]{:S(2)}) copy-start(f32[32,32,512]{2,1,0:T(8,128)S(1)} %all-to-all-done.1) | copy-start | bytes 6291460
  147.8 61.8 %all-to-all-start.2 = ((f32[32,32,512]{2,1,0:T(8,128)}), f32[32,32,512]{2,1,0:T(8,128)}, u32[]{:S(2)}, u32[]{:S(2)}) async-start(f32[32,32,512]{2,1,0:T(8,128)} %get-tuple-element.39), calls=%async_computation.2 | async-start | bytes 4194304 | tf_op jit(solution)/shard_map/all_to_all | solution.py:49
  198.3 6.2 %copy-start.6 = (f32[1024,512]{1,0:T(8,128)}, f32[1024,512]{1,0:T(8,128)S(1)}, u32[]{:S(2)}) copy-start(f32[1024,512]{1,0:T(8,128)S(1)} %bitcast_subtract_fusion) | copy-start | bytes 6291460
  209.6 10.1 %copy-start.13 = (s32[1,33]{1,0:T(1,128)S(1)}, s32[1,33]{1,0:T(1,128)}, u32[]{:S(2)}) copy-start(s32[1,33]{1,0:T(1,128)} %param.12) | copy-start | bytes 400
  209.6 43.8 %all-to-all-start.3 = ((f32[32,32,256]{2,1,0:T(8,128)}), f32[32,32,256]{2,1,0:T(8,128)}, u32[]{:S(2)}, u32[]{:S(2)}) async-start(f32[32,32,256]{2,1,0:T(8,128)} %get-tuple-element.48), calls=%async_computation.3 | async-start | bytes 2097152 | tf_op jit(solution)/shard_map/all_to_all | solution.py:49
  226.8 3.5 copy-start.9
  230.3 11.6 %copy-start.10 = (f32[384,512]{1,0:T(8,128)S(1)}, f32[384,512]{1,0:T(8,128)}, u32[]{:S(2)}) copy-start(f32[384,512]{1,0:T(8,128)} %fusion.30) | copy-start | bytes 2359300
  238.6 59.5 %collective-permute-start.4 = (f32[1024,384]{1,0:T(8,128)}, f32[1024,384]{1,0:T(8,128)}, u32[]{:S(2)}, u32[]{:S(2)}) collective-permute-start(f32[1024,384]{1,0:T(8,128)} %fusion.73), channel_id=1, source_target_pairs={{0,8},{8,16},{16,24},{24,56},{56,48},{48,40},{40,32},{32,64},{64,7... | collective-permute-start | bytes 4718600 | tf_op jit(solution)/shard_map/ppermute | solution.py:45
  249.9 48.3 %collective-permute-start.5 = (f32[1024,384]{1,0:T(8,128)}, f32[1024,384]{1,0:T(8,128)}, u32[]{:S(2)}, u32[]{:S(2)}) collective-permute-start(f32[1024,384]{1,0:T(8,128)} %fusion.74), channel_id=1, source_target_pairs={{8,0},{16,8},{24,16},{56,24},{48,56},{40,48},{32,40},{64,32},{72,6... | collective-permute-start | bytes 4718600 | tf_op jit(solution)/shard_map/ppermute | solution.py:45
  263.3 38.9 %all-to-all-start.4 = ((f32[32,32,256]{2,1,0:T(8,128)}), f32[32,32,256]{2,1,0:T(8,128)S(1)}, u32[]{:S(2)}, u32[]{:S(2)}) async-start(f32[32,32,256]{2,1,0:T(8,128)} %bitcast.80), calls=%async_computation.4 | async-start | bytes 2097152 | tf_op jit(solution)/shard_map/all_to_all | solution.py:49
  280.2 6.8 %copy-start.7 = (f32[1024,512]{1,0:T(8,128)S(1)}, f32[1024,512]{1,0:T(8,128)}, u32[]{:S(2)}) copy-start(f32[1024,512]{1,0:T(8,128)} %copy-done.6) | copy-start | bytes 6291460
  302.3 79.5 %copy-start.1 = (f32[32,32768]{1,0:T(8,128)S(1)}, f32[32,32768]{1,0:T(8,128)}, u32[]{:S(2)}) copy-start(f32[32,32768]{1,0:T(8,128)} %x_ref.3) | copy-start | bytes 12582916

commit v2 on v1

--- a/solution.py
+++ b/solution.py
@@ -13,6 +13,7 @@
 BOTH = ("member", "region")
 
 highest = lax.Precision.HIGHEST
+high = lax.Precision.HIGH
 f32 = jnp.float32
 in_vmem = pl.BlockSpec(memory_space=pltpu.VMEM)
 in_smem = pl.BlockSpec(memory_space=pltpu.SMEM)
@@ -173,12 +174,54 @@
     )(core, x, mid, rim)
 
 
+def hold_kernel(in_ref, out_ref):
+    out_ref[0] = in_ref[0]
+    out_ref[1] = in_ref[1]
+
+
+def hold(starts):
+    return pl.pallas_call(
+        hold_kernel,
+        in_specs=[in_smem],
+        out_specs=in_smem,
+        out_shape=jax.ShapeDtypeStruct((2,), jnp.int32),
+        cost_estimate=pl.CostEstimate(flops=10**11, bytes_accessed=8, transcendentals=0),
+    )(starts)
+
+
+def choose_kernel(starts_ref, own_ref, head_ref, tail_ref, out_ref):
+    for j in range(HALF):
+        at = slice(j * PIECE, (j + 1) * PIECE)
+        out_ref[:, at] = jnp.where(j < starts_ref[0], head_ref[:, at], own_ref[:, at])
+        to = slice((HALF + j) * PIECE, (HALF + j + 1) * PIECE)
+        out_ref[:, to] = jnp.where(j + 5 >= starts_ref[1], tail_ref[:, at], own_ref[:, to])
+
+
+def choose(starts, own, head, tail):
+    rows = own.shape[0] // 4
+    return pl.pallas_call(
+        choose_kernel,
+        grid=(4,),
+        in_specs=[in_smem] + [pl.BlockSpec((rows, w), lambda i: (i, 0)) for w in (768, 384, 384)],
+        out_specs=pl.BlockSpec((rows, 768), lambda i: (i, 0)),
+        out_shape=jax.ShapeDtypeStruct(own.shape, f32),
+        compiler_params=pltpu.CompilerParams(vmem_limit_bytes=60 * 2**20),
+        cost_estimate=pl.CostEstimate(flops=2**20, bytes_accessed=9 * 2**20, transcendentals=0),
+    )(starts, own, head, tail)
+
+
+def added(terms):
+    while len(terms) > 1:
+        terms = [x + y for x, y in zip(terms[::2], terms[1::2])]
+    return terms[0]
+
+
 def factor_block(a_ref, m_ref):
     n = PIECE
     row = lax.broadcasted_iota(jnp.int32, (8, n), 0)
+    p = a_ref[:8, :]
+    q = m_ref[:8, :]
     for lo in range(0, n, 8):
-        p = a_ref[lo : lo + 8, :]
-        q = m_ref[lo : lo + 8, :]
         b = [jnp.broadcast_to(p[:, lo + i : lo + i + 1], (8, n)) for i in range(8)]
         d = jnp.ones((8, n), f32)
         for i in range(8):
@@ -194,10 +237,16 @@
         u = p * s
         v = q * s
         m_ref[lo : lo + 8, :] = v
-        if lo + 8 < n:
-            step = dot(u.T, jnp.concatenate([u, v], axis=1), 1, 0)
-            a_ref[lo + 8 :, :] = a_ref[lo + 8 :, :] - step[lo + 8 :, :n]
-            m_ref[lo + 8 :, :] = m_ref[lo + 8 :, :] - step[lo + 8 :, n:]
+        at = lo + 8
+        if at < n:
+            turned = u.T
+            cols = [jnp.broadcast_to(turned[at : at + 8, i : i + 1], (8, n)) for i in range(8)]
+            p = a_ref[at : at + 8, :] - added([cols[i] * jnp.broadcast_to(u[i : i + 1, :], (8, n)) for i in range(8)])
+            q = m_ref[at : at + 8, :] - added([cols[i] * jnp.broadcast_to(v[i : i + 1, :], (8, n)) for i in range(8)])
+        if at + 8 < n:
+            step = dot(turned, jnp.concatenate([u, v], axis=1), 1, 0)
+            a_ref[at + 8 :, :] = a_ref[at + 8 :, :] - step[at + 8 :, :n]
+            m_ref[at + 8 :, :] = m_ref[at + 8 :, :] - step[at + 8 :, n:]
 
 
 def factor_kernel(c_ref, t_ref, a_ref, d_ref, m_ref):
@@ -288,51 +337,52 @@
     cover = lax.dynamic_slice_in_dim(cover, 8 * mine, 14, 0)
     cover = jnp.broadcast_to(cover[:, :, None], (14, OBS_PER, PIECE)).reshape(14, LOCAL)
     starts = lax.dynamic_slice_in_dim(window_piece_offsets[0], mine, 2, 0) - 8 * mine
-    block = lax.broadcasted_iota(jnp.int32, (1, 384), 1) // PIECE
-
-    rim = whole(rim)
-    head, tail = rim[:, :384], rim[:, 384:]
+
+    def centre(x):
+        return x - jnp.mean(x, axis=0, keepdims=True)
+
     rim, pred_s = in_order(rim, pred_s)
     pred = exchange(pred_s)
-    beyond = along_snake(head, -1)
-    ahead = along_snake(tail, 1)
-
-    pred, innov_s = in_order(pred, innov_s)
+    rim = centre(whole(rim))
+    head_far = along_snake(rim[:, :384], -1)
+    tail_far = along_snake(rim[:, 384:], 1)
+
+    pred, innov_s, rim = in_order(pred, innov_s, rim)
     innov = exchange(innov_s)
-    pred = whole(pred)
-    perturbed = pred - jnp.mean(pred, axis=0, keepdims=True)
+    perturbed = centre(whole(pred))
     cov = dot(perturbed, perturbed, 0, 0) / (members - 1.0)
     cov = cov + jnp.eye(LOCAL, dtype=f32) * var_rows[:1]
     root = inverse_factor(cov)
 
-    def gain(x, lo):
-        count = x.shape[1] // PIECE
-        centred = x - jnp.mean(x, axis=0, keepdims=True)
-        g = dot(centred, perturbed, 0, 0) / (members - 1.0)
-        g = g.reshape(count, PIECE, LOCAL) * cover[lo : lo + count, None, :]
-        return g.reshape(count * PIECE, LOCAL)
-
-    root, beyond, ahead = in_order(root, beyond, ahead)
-    beyond_gain = gain(beyond, 11)
-    ahead_gain = gain(ahead, 0)
-
-    innov, root, mid_s, beyond_gain, ahead_gain = in_order(innov, root, mid_s, beyond_gain, ahead_gain)
+    def gain(x, marks):
+        g = lax.dot_general(
+            x, perturbed, (((0,), (0,)), ((), ())), precision=high, preferred_element_type=f32
+        ) / (members - 1.0)
+        return (g.reshape(-1, PIECE, LOCAL) * marks[:, None, :]).reshape(-1, LOCAL)
+
+    root, rim, head_far, tail_far = in_order(root, rim, head_far, tail_far)
+    rim_gain = gain(rim, jnp.concatenate([cover[3:6], cover[8:11]]))
+    rim_gain, head_far, tail_far = in_order(rim_gain, head_far, tail_far)
+    head_gain = gain(head_far, cover[11:])
+    tail_gain = gain(tail_far, cover[:3])
+
+    innov, root, mid_s, rim_gain, head_gain, tail_gain = in_order(
+        innov, root, mid_s, rim_gain, head_gain, tail_gain
+    )
     mid = exchange(mid_s)
     weights = dot(root, dot(root, whole(innov), 1, 1), 0, 0)
-    beyond_inc = dot(weights, beyond_gain, 0, 1)
-    ahead_inc = dot(weights, ahead_gain, 0, 1)
-    head_back = along_snake(beyond_inc, 1)
-    tail_back = along_snake(ahead_inc, -1)
-    mid, beyond_inc, ahead_inc = in_order(mid, beyond_inc, ahead_inc)
-    mid_inc = dot(weights, gain(whole(mid), 6), 0, 1)
+    head_inc = dot(weights, head_gain, 0, 1)
+    tail_inc = dot(weights, tail_gain, 0, 1)
+    head_back = along_snake(head_inc, 1)
+    tail_back = along_snake(tail_inc, -1)
+    mid, head_inc, tail_inc = in_order(mid, head_inc, tail_inc)
+    mid_inc = dot(weights, gain(centre(whole(mid)), cover[6:8]), 0, 1)
     mid_out = exchange(in_parts(mid_inc))
-    mid_inc, late_weights, head, tail = in_order(mid_inc, weights, head, tail)
-    head_own = dot(late_weights, gain(head, 3), 0, 1)
-    tail_own = dot(late_weights, gain(tail, 8), 0, 1)
-    head_own, tail_own, head_back, tail_back = in_order(head_own, tail_own, head_back, tail_back)
-    head_inc = jnp.where(block < starts[0], head_back, head_own)
-    tail_inc = jnp.where(block + 5 >= starts[1], tail_back, tail_own)
-    rim_inc = jnp.concatenate([head_inc, tail_inc], axis=1)
+    mid_inc, starts = in_order(mid_inc, starts)
+    starts, late_weights = in_order(hold(starts), weights)
+    rim_inc = dot(late_weights, rim_gain, 0, 1)
+    rim_inc, head_back, tail_back = in_order(rim_inc, head_back, tail_back)
+    rim_inc = choose(starts, rim_inc, head_back, tail_back)
     mid_out, rim_inc = in_order(mid_out, rim_inc)
     rim_out = exchange(in_parts(rim_inc))
     return finish(core_word, background_realizations, mid_out, rim_out)

time: 390 us -> 384 us (0.985)
  waiting for transfers between devices: 105 us -> 122 us
  matrix products: 70.5 us -> 60.5 us
  other arithmetic: 13.7 us -> 6.83 us
  Pallas kernels: 49.6 us -> 43.9 us
    dot_general x13 -> x7, matrix products: 70.5 us -> 45.8 us  [dot(): lax.dot_general(a, b, (((da,), (db,)), ((), ())), precision=highest, pref...]
    dot_general x0 -> x4, matrix products: none -> 14.8 us  [gain(): lax.dot_general(x, perturbed, (((0,), (0,)), ((), ())), precision=high, p...]
    pallas_call x1, Pallas kernels: 37.4 us -> 25.6 us  [inverse_factor(): pl.pallas_call(factor_kernel, in_specs=[in_vmem], out_specs=in_vmem, out_...]
    ppermute x4, waiting for transfers between devices: 0.01 us -> 10.6 us  [along_snake(): return lax.ppermute(x, BOTH, route)]
    all_to_all x5, waiting for transfers between devices: 103 us -> 109 us  [exchange(): return lax.all_to_all(x, 'member', split_axis=0, concat_axis=0, tiled=True)]
    pallas_call x0 -> x2, Pallas kernels: none -> 6.03 us  [the longest x1 4.85 us: choose(): pl.pallas_call(choose_kernel, grid=(4,), in_specs=[in_smem] + [pl.BlockSp...]
    reduce_sum x6 -> x3, other arithmetic: 7.89 us -> 3.71 us  [centre(): return x - jnp.mean(x, axis=0, keepdims=True)]
  transfers between devices with their start and end apart: 11 -> 11, of which waited for: 3 -> 5; matrix products, arithmetic and copies ran while one was open for 23% -> 19% of each run, Pallas kernels for 11% -> 10%
where the time goes in v2:
time: 384 us; the launch traced here: 380 us
  waiting for transfers between devices  122 us (32%)
  blocking collectives  82.3 us (21%)
  matrix products  60.5 us (16%)
  starting transfers between devices  55.9 us (15%)
  Pallas kernels  43.9 us (11%)
  local copies, waits for them, and re-layouts  7.85 us (2%)
  other arithmetic  6.83 us (2%)
    all_to_all x5, waiting for transfers between devices, exchange(): return lax.all_to_all(x, 'member', split_axis=0, concat_axis=0, tiled=True)  109 us
    all_to_all x1, blocking collectives, exchange(): return lax.all_to_all(x, 'member', split_axis=0, concat_axis=0, tiled=True)  82.3 us
    dot_general x7, matrix products, dot(): lax.dot_general(a, b, (((da,), (db,)), ((), ())), precision=highest, pref...  45.8 us
    all_to_all x5, starting transfers between devices, exchange(): return lax.all_to_all(x, 'member', split_axis=0, concat_axis=0, tiled=True)  41.3 us
    pallas_call x1, Pallas kernels, inverse_factor(): pl.pallas_call(factor_kernel, in_specs=[in_vmem], out_specs=in_vmem, out_...  25.6 us
    dot_general x4, matrix products, gain(): lax.dot_general(x, perturbed, (((0,), (0,)), ((), ())), precision=high, p...  14.8 us
    ppermute x4, starting transfers between devices, along_snake(): return lax.ppermute(x, BOTH, route)  12.8 us
    ppermute x4, waiting for transfers between devices, along_snake(): return lax.ppermute(x, BOTH, route)  10.6 us
  transfers between devices with their start and end apart: 11, of which 5 were waited for; matrix products, arithmetic and copies ran while one was open for 19% of the time, Pallas kernels for 10%

profile of v2, /device:TPU:12, one launch (start us, length us, event | category | flops | bytes accessed | tf_op | source)
XLA Modules:
  0.0 380.2 jit_solution(9377063981707239487)
XLA Ops:
  0.0 2.2 copy-done
  2.2 3.7 shard_map.82
  5.9 0.0 copy-start.5
  5.9 11.9 %all-to-all-start = ((f32[32,32,768]{2,1,0:T(8,128)}), f32[32,32,768]{2,1,0:T(8,128)}, u32[]{:S(2)}, u32[]{:S(2)}) async-start(f32[32,32,768]{2,1,0:T(8,128)} %get-tuple-element.39), calls=%async_computation | async-start | bytes 6291456 | tf_op jit(solution)/shard_map/all_to_all | solution.py:50
  17.9 0.6 shard_map.83
  18.5 0.0 collective-permute-start
  18.5 1.7 collective-permute-start.1
  20.2 0.1 copy.9.lists_ref
  20.3 0.1 pad_add_fusion.place_ref
  20.4 2.7 collective-permute-done.before_ref
  23.0 4.0 %shard_map.84 = (f32[32,32,512]{2,1,0:T(8,128)}, f32[32,32,512]{2,1,0:T(8,128)}, f32[8,512]{1,0:T(8,128)S(1)}) custom-call(s32[2]{0:T(128)S(1)} %pad_add_fusion.place_ref, s32[32,4]{1,0:T(8,128)S(1)} %copy.9.lists_ref, f32[32,4096]{1,0:T(8,128)S(1)} %copy-done.2, f32[32,4096]{1,0:T(8,128)S(1)} %copy-done.3, f32[1,4096]{1,0:T(1,128)S(1)} %bitcast.76, ...), custom_call_target="tpu_custom_call" | custom-call | bytes 6291456 | tf_op jit(solution)/shard_map/pallas_call | solution.py:135
  27.1 62.0 %all-to-all-done = f32[32,32,768]{2,1,0:T(8,128)} async-done(((f32[32,32,768]{2,1,0:T(8,128)}), f32[32,32,768]{2,1,0:T(8,128)}, u32[]{:S(2)}, u32[]{:S(2)}) %all-to-all-start) | async-done | bytes 3145760 | tf_op jit(solution)/shard_map/all_to_all | solution.py:50
  89.1 7.5 %all-to-all-start.1 = ((f32[32,32,512]{2,1,0:T(8,128)}), f32[32,32,512]{2,1,0:T(8,128)S(1)}, u32[]{:S(2)}, u32[]{:S(2)}) async-start(f32[32,32,512]{2,1,0:T(8,128)} %get-tuple-element.43), calls=%async_computation.1 | async-start | bytes 4194304 | tf_op jit(solution)/shard_map/all_to_all | solution.py:50
  96.6 0.1 pad_dynamic-slice_fusion
  96.7 0.1 fusion.29
  96.8 0.1 copy.11
  96.9 0.1 copy.10
  97.0 0.1 copy.12
  97.1 0.1 broadcast_bitcast_fusion.1
  97.1 0.1 copy.13
  97.2 0.1 broadcast_bitcast_fusion
  97.3 0.1 broadcast_bitcast_fusion.2
  97.4 0.1 broadcast_bitcast_fusion.3
  97.5 2.1 reduce_sum.27
  99.6 2.1 bitcast_subtract_fusion
  101.7 2.1 fusion.28
  103.8 0.6 copy-done.6
  104.4 2.1 collective-permute-start.2
  106.5 3.7 collective-permute-start.3
  110.2 37.6 %all-to-all-done.1 = f32[32,32,512]{2,1,0:T(8,128)S(1)} async-done(((f32[32,32,512]{2,1,0:T(8,128)}), f32[32,32,512]{2,1,0:T(8,128)S(1)}, u32[]{:S(2)}, u32[]{:S(2)}) %all-to-all-start.1) | async-done | bytes 2097184 | tf_op jit(solution)/shard_map/all_to_all | solution.py:50
  147.8 5.8 %all-to-all-start.2 = ((f32[32,32,512]{2,1,0:T(8,128)}), f32[32,32,512]{2,1,0:T(8,128)}, u32[]{:S(2)}, u32[]{:S(2)}) async-start(f32[32,32,512]{2,1,0:T(8,128)} %get-tuple-element.46), calls=%async_computation.2 | async-start | bytes 4194304 | tf_op jit(solution)/shard_map/all_to_all | solution.py:50
  153.6 0.2 reduce_sum.28
  153.8 3.6 fusion.10.c_ref
  157.4 25.6 %shard_map.85 = f32[512,512]{1,0:T(8,128)S(1)} custom-call(f32[512,512]{1,0:T(8,128)S(1)} %fusion.10.c_ref), custom_call_target="tpu_custom_call" | custom-call | flops 35999997952 | bytes 2097152 | tf_op jit(solution)/shard_map/pallas_call | solution.py:273
  183.0 0.0 copy-start.7
  183.1 0.3 bitcast_subtract_fusion.1
  183.4 1.6 copy-done.7
  184.9 3.9 %bitcast_multiply_fusion = f32[768,512]{1,0:T(8,128)} fusion(f32[1024,768]{1,0:T(8,128)S(1)} %copy-done.7, f32[1024,512]{1,0:T(8,128)S(1)} %bitcast_subtract_fusion.1, f32[6,512]{1,0:T(8,128)S(1)} %pad_maximum_fusion), kind=kOutput, calls=%fused_computation.6 | convolution fusion | flops 2416705536 | bytes 6828032 | tf_op jit(solution)/shard_map/dot_general | solution.py:358
  188.8 0.1 mul.80
  188.9 4.0 %fusion.13 = f32[384,512]{1,0:T(8,128)} fusion(f32[384,512]{1,0:T(8,128)S(1)} %bitcast.81, f32[1024,384]{1,0:T(8,128)} %collective-permute-done.2, f32[1024,512]{1,0:T(8,128)S(1)} %bitcast_subtract_fusion.1), kind=kOutput, calls=%fused_computation.12 | convolution fusion | flops 1208352768 | bytes 5242880 | tf_op jit(solution)/shard_map/dot_general | solution.py:358
  192.9 0.1 mul.84
  193.0 3.9 %fusion.14 = f32[384,512]{1,0:T(8,128)} fusion(f32[384,512]{1,0:T(8,128)S(1)} %bitcast.80, f32[1024,384]{1,0:T(8,128)} %collective-permute-done.3, f32[1024,512]{1,0:T(8,128)S(1)} %bitcast_subtract_fusion.1), kind=kOutput, calls=%fused_computation.13 | convolution fusion | flops 1208352768 | bytes 5242880 | tf_op jit(solution)/shard_map/dot_general | solution.py:358
  196.9 9.5 %all-to-all-done.2 = f32[32,32,512]{2,1,0:T(8,128)} async-done(((f32[32,32,512]{2,1,0:T(8,128)}), f32[32,32,512]{2,1,0:T(8,128)}, u32[]{:S(2)}, u32[]{:S(2)}) %all-to-all-start.2) | async-done | bytes 2097184 | tf_op jit(solution)/shard_map/all_to_all | solution.py:50
  206.4 7.2 %all-to-all-start.3 = ((f32[32,32,256]{2,1,0:T(8,128)}), f32[32,32,256]{2,1,0:T(8,128)}, u32[]{:S(2)}, u32[]{:S(2)}) async-start(f32[32,32,256]{2,1,0:T(8,128)} %get-tuple-element.60), calls=%async_computation.3 | async-start | bytes 2097152 | tf_op jit(solution)/shard_map/all_to_all | solution.py:50
  213.6 0.1 slice.47
  213.7 0.1 copy.14
  213.8 0.1 broadcast_bitcast_fusion.4
  213.9 0.7 subtract_bitcast_fusion.in_ref
  214.6 5.2 %fusion.30 = f32[512,1024]{1,0:T(8,128)S(1)} fusion(f32[512,512]{1,0:T(8,128)S(1)} %shard_map.85, f32[1024,512]{1,0:T(8,128)} %bitcast.13), kind=kOutput, calls=%fused_computation.42 | convolution fusion | flops 3221225472 | bytes 5242880 | tf_op jit(solution)/shard_map/dot_general | solution.py:23
  219.7 3.5 fusion.31
  223.3 8.2 %fusion.32 = f32[1024,384]{1,0:T(8,128)} fusion(f32[512,1024]{1,0:T(8,128)S(1)} %fusion.31, f32[384,512]{1,0:T(8,128)S(1)} %copy-done.10), kind=kOutput, calls=%fused_computation.44 | convolution fusion | flops 2415919104 | bytes 4456448 | tf_op jit(solution)/shard_map/dot_general | solution.py:23
  231.5 3.4 collective-permute-start.4
  234.9 7.8 %fusion.33 = f32[1024,384]{1,0:T(8,128)} fusion(f32[512,1024]{1,0:T(8,128)S(1)} %fusion.31, f32[384,512]{1,0:T(8,128)S(1)} %copy-done.9), kind=kOutput, calls=%fused_computation.45 | convolution fusion | flops 2415919104 | bytes 4456448 | tf_op jit(solution)/shard_map/dot_general | solution.py:23
  242.7 3.6 collective-permute-start.5
  246.4 1.4 reduce_sum.29
  247.8 3.0 fusion.21
  250.8 4.4 %fusion.34 = f32[1024,256]{1,0:T(8,128)} fusion(f32[512,1024]{1,0:T(8,128)S(1)} %fusion.31, f32[256,512]{1,0:T(8,128)S(1)} %fusion.21), kind=kOutput, calls=%fused_computation.46 | convolution fusion | flops 1610612736 | bytes 3670016 | tf_op jit(solution)/shard_map/dot_general | solution.py:23
  255.3 8.9 %all-to-all-start.4 = ((f32[32,32,256]{2,1,0:T(8,128)}), f32[32,32,256]{2,1,0:T(8,128)S(1)}, u32[]{:S(2)}, u32[]{:S(2)}) async-start(f32[32,32,256]{2,1,0:T(8,128)} %bitcast.79), calls=%async_computation.4 | async-start | bytes 2097152 | tf_op jit(solution)/shard_map/all_to_all | solution.py:50
  264.2 1.2 shard_map.86.starts_ref
  265.3 13.0 %fusion.35.own_ref = f32[1024,768]{1,0:T(8,128)} fusion(f32[512,1024]{1,0:T(8,128)S(1)} %fusion.31, f32[768,512]{1,0:T(8,128)} %bitcast_multiply_fusion), kind=kOutput, calls=%fused_computation.47 | convolution fusion | flops 4831838208 | bytes 6815744 | tf_op jit(solution)/shard_map/dot_general | solution.py:23
  278.3 10.6 %collective-permute-done.5.tail_ref = f32[1024,384]{1,0:T(8,128)} collective-permute-done((f32[1024,384]{1,0:T(8,128)}, f32[1024,384]{1,0:T(8,128)}, u32[]{:S(2)}, u32[]{:S(2)}) %collective-permute-start.5) | collective-permute-done | bytes 1572896 | tf_op jit(solution)/shard_map/ppermute | solution.py:46
  288.9 4.8 %shard_map.87 = f32[1024,768]{1,0:T(8,128)} custom-call(s32[2]{0:T(128)} %shard_map.86.starts_ref, f32[1024,768]{1,0:T(8,128)} %fusion.35.own_ref, f32[1024,384]{1,0:T(8,128)} %collective-permute-done.4.head_ref, f32[1024,384]{1,0:T(8,128)} %collective-permute-done.5.tail_ref), custom_call_target="tpu_custom_call" | custom-call | flops 1048576 | bytes 9437184 | tf_op jit(solution)/shard_map/pallas_call | solution.py:202
  293.8 82.3 %all_to_all.30.rim_ref = f32[32,32,768]{2,1,0:T(8,128)S(1)} all-to-all(f32[32,32,768]{2,1,0:T(8,128)} %bitcast.78), channel_id=1, replica_groups=mesh['member'=32,'region'=8] {'member'}, dimensions={0} | all-to-all | bytes 6291456 | tf_op jit(solution)/shard_map/all_to_all | solution.py:50
  376.1 3.9 %shard_map.88 = f32[32,32768]{1,0:T(8,128)} custom-call(s32[1]{0:T(128)} %bitcast.core_ref, f32[32,32768]{1,0:T(8,128)S(1)} %copy-done.1, f32[32,32,256]{2,1,0:T(8,128)S(1)} %all-to-all-done.4.mid_ref, f32[32,32,768]{2,1,0:T(8,128)S(1)} %all_to_all.30.rim_ref), custom_call_target="tpu_custom_call" | custom-call | flops 1048576 | bytes 12582912 | tf_op jit(solution)/shard_map/pallas_call | solution.py:161
  (40 shorter events, 0.2 us)
Async XLA Ops:
  0.0 2.2 copy-start
  5.9 11.9 %copy-start.2 = (f32[32,4096]{1,0:T(8,128)S(1)}, f32[32,4096]{1,0:T(8,128)}, u32[]{:S(2)}) copy-start(f32[32,4096]{1,0:T(8,128)} %pred_ref.3) | copy-start | bytes 1572868
  5.9 11.9 %copy-start.3 = (f32[32,4096]{1,0:T(8,128)S(1)}, f32[32,4096]{1,0:T(8,128)}, u32[]{:S(2)}) copy-start(f32[32,4096]{1,0:T(8,128)} %innov_ref.3) | copy-start | bytes 1572868
  5.9 12.0 %copy-start.4 = (f32[4096]{0:T(1024)S(1)}, f32[4096]{0:T(1024)}, u32[]{:S(2)}) copy-start(f32[4096]{0:T(1024)} %param.11) | copy-start | bytes 49156
  5.9 12.0 %copy-start.5 = (s32[1,2,4]{2,1,0:T(2,128)S(1)}, s32[1,2,4]{2,1,0:T(2,128)}, u32[]{:S(2)}) copy-start(s32[1,2,4]{2,1,0:T(2,128)} %param.14) | copy-start | bytes 100
  5.9 14.3 %copy-start.12 = (s32[1,32,4]{1,2,0:T(4,128)S(1)}, s32[1,32,4]{1,2,0:T(4,128)}, u32[]{:S(2)}) copy-start(s32[1,32,4]{1,2,0:T(4,128)} %param.13) | copy-start | bytes 1540
  5.9 83.2 %all-to-all-start = ((f32[32,32,768]{2,1,0:T(8,128)}), f32[32,32,768]{2,1,0:T(8,128)}, u32[]{:S(2)}, u32[]{:S(2)}) async-start(f32[32,32,768]{2,1,0:T(8,128)} %get-tuple-element.39), calls=%async_computation | async-start | bytes 6291456 | tf_op jit(solution)/shard_map/all_to_all | solution.py:50
  18.5 4.6 %collective-permute-start = (f32[72,512]{1,0:T(8,128)S(1)}, f32[72,512]{1,0:T(8,128)S(1)}, u32[]{:S(2)}, u32[]{:S(2)}) collective-permute-start(f32[72,512]{1,0:T(8,128)S(1)} %get-tuple-element.40), channel_id=1, source_target_pairs={{0,1},{1,2},{2,3},{3,4},{4,5},{5,6},{6,7},{7,0},{8,9},{9,10},{10,1... | collective-permute-start | bytes 442376 | tf_op jit(solution)/shard_map/ppermute | solution.py:318
  18.5 4.6 %collective-permute-start.1 = (f32[72,512]{1,0:T(8,128)S(1)}, f32[72,512]{1,0:T(8,128)S(1)}, u32[]{:S(2)}, u32[]{:S(2)}) collective-permute-start(f32[72,512]{1,0:T(8,128)S(1)} %get-tuple-element.41), channel_id=1, source_target_pairs={{0,7},{1,0},{2,1},{3,2},{4,3},{5,4},{6,5},{7,6},{8,15},{9,8},{10,9... | collective-permute-start | bytes 442376 | tf_op jit(solution)/shard_map/ppermute | solution.py:319
  89.1 7.5 %copy-start.11 = (s32[1,256,4]{1,2,0:T(4,128)S(1)}, s32[1,256,4]{1,2,0:T(4,128)}, u32[]{:S(2)}) copy-start(s32[1,256,4]{1,2,0:T(4,128)} %param.15) | copy-start | bytes 12292
  89.1 58.7 %all-to-all-start.1 = ((f32[32,32,512]{2,1,0:T(8,128)}), f32[32,32,512]{2,1,0:T(8,128)S(1)}, u32[]{:S(2)}, u32[]{:S(2)}) async-start(f32[32,32,512]{2,1,0:T(8,128)} %get-tuple-element.43), calls=%async_computation.1 | async-start | bytes 4194304 | tf_op jit(solution)/shard_map/all_to_all | solution.py:50
  101.7 2.7 copy-start.6
  104.4 78.7 %collective-permute-start.2 = (f32[1024,384]{1,0:T(8,128)}, f32[1024,384]{1,0:T(8,128)}, u32[]{:S(2)}, u32[]{:S(2)}) collective-permute-start(f32[1024,384]{1,0:T(8,128)} %get-tuple-element.74), channel_id=1, source_target_pairs={{8,0},{16,8},{24,16},{56,24},{48,56},{40,48},{32,40},{64,32},{72,6... | collective-permute-start | bytes 4718600 | tf_op jit(solution)/shard_map/ppermute | solution.py:46
  106.5 76.5 %collective-permute-start.3 = (f32[1024,384]{1,0:T(8,128)}, f32[1024,384]{1,0:T(8,128)}, u32[]{:S(2)}, u32[]{:S(2)}) collective-permute-start(f32[1024,384]{1,0:T(8,128)} %get-tuple-element.73), channel_id=1, source_target_pairs={{0,8},{8,16},{16,24},{24,56},{56,48},{48,40},{40,32},{32,64},{64,7... | collective-permute-start | bytes 4718600 | tf_op jit(solution)/shard_map/ppermute | solution.py:46
  147.8 35.3 %copy-start.8 = (f32[32,32,512]{2,1,0:T(8,128)}, f32[32,32,512]{2,1,0:T(8,128)S(1)}, u32[]{:S(2)}) copy-start(f32[32,32,512]{2,1,0:T(8,128)S(1)} %all-to-all-done.1) | copy-start | bytes 6291460
  147.8 58.6 %all-to-all-start.2 = ((f32[32,32,512]{2,1,0:T(8,128)}), f32[32,32,512]{2,1,0:T(8,128)}, u32[]{:S(2)}, u32[]{:S(2)}) async-start(f32[32,32,512]{2,1,0:T(8,128)} %get-tuple-element.46), calls=%async_computation.2 | async-start | bytes 4194304 | tf_op jit(solution)/shard_map/all_to_all | solution.py:50
  183.0 1.9 copy-start.7
  196.9 17.0 %copy-start.13 = (s32[1,33]{1,0:T(1,128)S(1)}, s32[1,33]{1,0:T(1,128)}, u32[]{:S(2)}) copy-start(s32[1,33]{1,0:T(1,128)} %param.12) | copy-start | bytes 400
  206.4 40.0 %all-to-all-start.3 = ((f32[32,32,256]{2,1,0:T(8,128)}), f32[32,32,256]{2,1,0:T(8,128)}, u32[]{:S(2)}, u32[]{:S(2)}) async-start(f32[32,32,256]{2,1,0:T(8,128)} %get-tuple-element.60), calls=%async_computation.3 | async-start | bytes 2097152 | tf_op jit(solution)/shard_map/all_to_all | solution.py:50
  219.7 3.5 copy-start.10
  223.3 11.6 %copy-start.9 = (f32[384,512]{1,0:T(8,128)S(1)}, f32[384,512]{1,0:T(8,128)}, u32[]{:S(2)}) copy-start(f32[384,512]{1,0:T(8,128)} %fusion.14) | copy-start | bytes 2359300
  231.5 46.8 %collective-permute-start.4 = (f32[1024,384]{1,0:T(8,128)}, f32[1024,384]{1,0:T(8,128)}, u32[]{:S(2)}, u32[]{:S(2)}) collective-permute-start(f32[1024,384]{1,0:T(8,128)} %fusion.32), channel_id=1, source_target_pairs={{0,8},{8,16},{16,24},{24,56},{56,48},{48,40},{40,32},{32,64},{64,7... | collective-permute-start | bytes 4718600 | tf_op jit(solution)/shard_map/ppermute | solution.py:46
  242.7 46.2 %collective-permute-start.5 = (f32[1024,384]{1,0:T(8,128)}, f32[1024,384]{1,0:T(8,128)}, u32[]{:S(2)}, u32[]{:S(2)}) collective-permute-start(f32[1024,384]{1,0:T(8,128)} %fusion.33), channel_id=1, source_target_pairs={{8,0},{16,8},{24,16},{56,24},{48,56},{40,48},{32,40},{64,32},{72,6... | collective-permute-start | bytes 4718600 | tf_op jit(solution)/shard_map/ppermute | solution.py:46
  255.3 38.5 %all-to-all-start.4 = ((f32[32,32,256]{2,1,0:T(8,128)}), f32[32,32,256]{2,1,0:T(8,128)S(1)}, u32[]{:S(2)}, u32[]{:S(2)}) async-start(f32[32,32,256]{2,1,0:T(8,128)} %bitcast.79), calls=%async_computation.4 | async-start | bytes 2097152 | tf_op jit(solution)/shard_map/all_to_all | solution.py:50
  293.8 82.3 %copy-start.1 = (f32[32,32768]{1,0:T(8,128)S(1)}, f32[32,32768]{1,0:T(8,128)}, u32[]{:S(2)}) copy-start(f32[32,32768]{1,0:T(8,128)} %x_ref.3) | copy-start | bytes 12582916

commit v3 on v2

--- a/solution.py
+++ b/solution.py
@@ -1,3 +1,5 @@
+import functools
+
 import jax
 import jax.numpy as jnp
 from jax import lax
@@ -19,9 +21,9 @@
 in_smem = pl.BlockSpec(memory_space=pltpu.SMEM)
 
 
-def dot(a, b, da, db):
+def dot(a, b, da, db, precision=highest):
     return lax.dot_general(
-        a, b, (((da,), (db,)), ((), ())), precision=highest, preferred_element_type=f32
+        a, b, (((da,), (db,)), ((), ())), precision=precision, preferred_element_type=f32
     )
 
 
@@ -91,7 +93,7 @@
         in_specs=[in_smem, in_vmem, in_vmem, in_vmem],
         out_specs=[in_vmem, in_vmem],
         out_shape=[jax.ShapeDtypeStruct((rows, LOCAL), f32)] * 2,
-        compiler_params=pltpu.CompilerParams(vmem_limit_bytes=8 * 2**20),
+        compiler_params=pltpu.CompilerParams(vmem_limit_bytes=60 * 2**20),
         cost_estimate=pl.CostEstimate(flops=0, bytes_accessed=2**20, transcendentals=0),
     )(ids, pred, innov, var)
 
@@ -142,7 +144,7 @@
             pltpu.VMEM((members, own + 2 * LOCAL), f32),
             pltpu.VMEM((8, own + 2 * LOCAL), f32),
         ],
-        compiler_params=pltpu.CompilerParams(vmem_limit_bytes=24 * 2**20),
+        compiler_params=pltpu.CompilerParams(vmem_limit_bytes=60 * 2**20),
         cost_estimate=pl.CostEstimate(flops=0, bytes_accessed=6 * 2**20, transcendentals=0),
     )(place, lists, pred, innov, var, before, after)
 
@@ -189,25 +191,29 @@
     )(starts)
 
 
-def choose_kernel(starts_ref, own_ref, head_ref, tail_ref, out_ref):
+def choose_kernel(side, starts_ref, own_ref, back_ref, out_ref):
     for j in range(HALF):
         at = slice(j * PIECE, (j + 1) * PIECE)
-        out_ref[:, at] = jnp.where(j < starts_ref[0], head_ref[:, at], own_ref[:, at])
-        to = slice((HALF + j) * PIECE, (HALF + j + 1) * PIECE)
-        out_ref[:, to] = jnp.where(j + 5 >= starts_ref[1], tail_ref[:, at], own_ref[:, to])
-
-
-def choose(starts, own, head, tail):
-    rows = own.shape[0] // 4
-    return pl.pallas_call(
-        choose_kernel,
-        grid=(4,),
-        in_specs=[in_smem] + [pl.BlockSpec((rows, w), lambda i: (i, 0)) for w in (768, 384, 384)],
-        out_specs=pl.BlockSpec((rows, 768), lambda i: (i, 0)),
+        theirs = j < starts_ref[0] if side == 0 else j + 5 >= starts_ref[1]
+        out_ref[:, at] = jnp.where(theirs, back_ref[:, at], own_ref[:, at])
+
+
+def choose(side, starts, own, back):
+    rows, width = own.shape[0] // 2, HALF * PIECE
+    return pl.pallas_call(
+        functools.partial(choose_kernel, side),
+        grid=(2,),
+        in_specs=[
+            in_smem,
+            pl.BlockSpec((rows, width), lambda i: (i, side)),
+            pl.BlockSpec((rows, width), lambda i: (i, 0)),
+        ],
+        out_specs=pl.BlockSpec((rows, width), lambda i: (i, side)),
         out_shape=jax.ShapeDtypeStruct(own.shape, f32),
+        input_output_aliases={1: 0},
         compiler_params=pltpu.CompilerParams(vmem_limit_bytes=60 * 2**20),
-        cost_estimate=pl.CostEstimate(flops=2**20, bytes_accessed=9 * 2**20, transcendentals=0),
-    )(starts, own, head, tail)
+        cost_estimate=pl.CostEstimate(flops=2**20, bytes_accessed=5 * 2**20, transcendentals=0),
+    )(starts, own, back)
 
 
 def added(terms):
@@ -355,34 +361,39 @@
     root = inverse_factor(cov)
 
     def gain(x, marks):
-        g = lax.dot_general(
-            x, perturbed, (((0,), (0,)), ((), ())), precision=high, preferred_element_type=f32
-        ) / (members - 1.0)
+        g = dot(x, perturbed, 0, 0, high) / (members - 1.0)
         return (g.reshape(-1, PIECE, LOCAL) * marks[:, None, :]).reshape(-1, LOCAL)
+
+    def solved(g):
+        return dot(root, dot(root, g, 1, 1), 0, 0)
 
     root, rim, head_far, tail_far = in_order(root, rim, head_far, tail_far)
     rim_gain = gain(rim, jnp.concatenate([cover[3:6], cover[8:11]]))
     rim_gain, head_far, tail_far = in_order(rim_gain, head_far, tail_far)
-    head_gain = gain(head_far, cover[11:])
-    tail_gain = gain(tail_far, cover[:3])
-
-    innov, root, mid_s, rim_gain, head_gain, tail_gain = in_order(
-        innov, root, mid_s, rim_gain, head_gain, tail_gain
+    head_solved = solved(gain(head_far, cover[11:]))
+    tail_solved = solved(gain(tail_far, cover[:3]))
+
+    innov, root, mid_s, rim_gain, head_solved, tail_solved = in_order(
+        innov, root, mid_s, rim_gain, head_solved, tail_solved
     )
     mid = exchange(mid_s)
-    weights = dot(root, dot(root, whole(innov), 1, 1), 0, 0)
-    head_inc = dot(weights, head_gain, 0, 1)
-    tail_inc = dot(weights, tail_gain, 0, 1)
+    innov = whole(innov)
+    head_inc = dot(innov, head_solved, 1, 0, high)
+    tail_inc = dot(innov, tail_solved, 1, 0, high)
     head_back = along_snake(head_inc, 1)
     tail_back = along_snake(tail_inc, -1)
-    mid, head_inc, tail_inc = in_order(mid, head_inc, tail_inc)
+    innov, head_inc, tail_inc = in_order(innov, head_inc, tail_inc)
+    weights = dot(root, dot(root, innov, 1, 1), 0, 0)
+    mid, weights = in_order(mid, weights)
     mid_inc = dot(weights, gain(centre(whole(mid)), cover[6:8]), 0, 1)
     mid_out = exchange(in_parts(mid_inc))
     mid_inc, starts = in_order(mid_inc, starts)
     starts, late_weights = in_order(hold(starts), weights)
     rim_inc = dot(late_weights, rim_gain, 0, 1)
-    rim_inc, head_back, tail_back = in_order(rim_inc, head_back, tail_back)
-    rim_inc = choose(starts, rim_inc, head_back, tail_back)
+    rim_inc, head_back = in_order(rim_inc, head_back)
+    rim_inc = choose(0, starts, rim_inc, head_back)
+    rim_inc, tail_back = in_order(rim_inc, tail_back)
+    rim_inc = choose(1, starts, rim_inc, tail_back)
     mid_out, rim_inc = in_order(mid_out, rim_inc)
     rim_out = exchange(in_parts(rim_inc))
     return finish(core_word, background_realizations, mid_out, rim_out)

time: 384 us -> 375 us (0.977)
  waiting for transfers between devices: 122 us -> 115 us
  blocking collectives: 82.3 us -> 77.5 us
    ppermute x4, waiting for transfers between devices: 10.6 us -> 0.01 us  [along_snake(): return lax.ppermute(x, BOTH, route)]
    all_to_all x1, blocking collectives: 82.3 us -> 77.5 us  [exchange(): return lax.all_to_all(x, 'member', split_axis=0, concat_axis=0, tiled=True)]
    all_to_all x5, waiting for transfers between devices: 109 us -> 114 us  [exchange(): return lax.all_to_all(x, 'member', split_axis=0, concat_axis=0, tiled=True)]
    dot_general x11 -> x15, matrix products: 60.5 us -> 59.6 us  [dot(): lax.dot_general(a, b, (((da,), (db,)), ((), ())), precision=precision, pr...]
where the time goes in v3:
time: 375 us; the launch traced here: 371 us
  waiting for transfers between devices  115 us (31%)
  blocking collectives  77.5 us (21%)
  matrix products  59.6 us (16%)
  starting transfers between devices  55.3 us (15%)
  Pallas kernels  46.5 us (12%)
  local copies, waits for them, and re-layouts  9.37 us (2%)
  other arithmetic  6.84 us (2%)
    all_to_all x5, waiting for transfers between devices, exchange(): return lax.all_to_all(x, 'member', split_axis=0, concat_axis=0, tiled=True)  114 us
    all_to_all x1, blocking collectives, exchange(): return lax.all_to_all(x, 'member', split_axis=0, concat_axis=0, tiled=True)  77.5 us
    dot_general x15, matrix products, dot(): lax.dot_general(a, b, (((da,), (db,)), ((), ())), precision=precision, pr...  59.6 us
    all_to_all x5, starting transfers between devices, exchange(): return lax.all_to_all(x, 'member', split_axis=0, concat_axis=0, tiled=True)  40.4 us
    pallas_call x1, Pallas kernels, inverse_factor(): pl.pallas_call(factor_kernel, in_specs=[in_vmem], out_specs=in_vmem, out_...  25.6 us
    ppermute x4, starting transfers between devices, along_snake(): return lax.ppermute(x, BOTH, route)  13.2 us
  transfers between devices with their start and end apart: 11, of which 5 were waited for; matrix products, arithmetic and copies ran while one was open for 19% of the time, Pallas kernels for 10%

profile of v3, /device:TPU:12, one launch (start us, length us, event | category | flops | bytes accessed | tf_op | source)
XLA Modules:
  0.0 371.1 jit_solution(8729776367244591155)
XLA Ops:
  0.0 2.2 copy-done
  2.2 3.7 shard_map.82
  5.9 11.8 %all-to-all-start = ((f32[32,32,768]{2,1,0:T(8,128)}), f32[32,32,768]{2,1,0:T(8,128)S(1)}, u32[]{:S(2)}, u32[]{:S(2)}) async-start(f32[32,32,768]{2,1,0:T(8,128)} %get-tuple-element.42), calls=%async_computation | async-start | bytes 6291456 | tf_op jit(solution)/shard_map/all_to_all | solution.py:52
  17.7 2.0 shard_map.83
  19.7 1.7 collective-permute-start.1
  21.4 0.7 copy.11.lists_ref
  22.1 0.6 pad_add_fusion.place_ref
  22.7 1.8 collective-permute-done.before_ref
  24.5 0.6 copy-done.5
  25.1 0.7 copy-done.6
  25.8 4.5 %shard_map.84 = (f32[32,32,512]{2,1,0:T(8,128)}, f32[32,32,512]{2,1,0:T(8,128)}, f32[8,512]{1,0:T(8,128)}) custom-call(s32[2]{0:T(128)} %pad_add_fusion.place_ref, s32[32,4]{1,0:T(8,128)} %copy.11.lists_ref, f32[32,4096]{1,0:T(8,128)} %pred_ref.3, f32[32,4096]{1,0:T(8,128)} %innov_ref.3, f32[1,4096]{1,0:T(1,128)} %bitcast.92, f32[72,512]{1,0:T(8,128)} %copy-done.5, ...), custom_call_target="tpu_custom_call" | custom-call | bytes 6291456 | tf_op jit(solution)/shard_map/pallas_call | solution.py:137
  30.3 58.6 %all-to-all-done = f32[32,32,768]{2,1,0:T(8,128)S(1)} async-done(((f32[32,32,768]{2,1,0:T(8,128)}), f32[32,32,768]{2,1,0:T(8,128)S(1)}, u32[]{:S(2)}, u32[]{:S(2)}) %all-to-all-start) | async-done | bytes 3145760 | tf_op jit(solution)/shard_map/all_to_all | solution.py:52
  89.0 7.5 %all-to-all-start.1 = ((f32[32,32,512]{2,1,0:T(8,128)}), f32[32,32,512]{2,1,0:T(8,128)}, u32[]{:S(2)}, u32[]{:S(2)}) async-start(f32[32,32,512]{2,1,0:T(8,128)} %get-tuple-element.46), calls=%async_computation.1 | async-start | bytes 4194304 | tf_op jit(solution)/shard_map/all_to_all | solution.py:52
  96.5 0.1 pad_dynamic-slice_fusion
  96.6 0.1 fusion.29
  96.7 0.1 copy.13
  96.8 0.1 copy.12
  96.9 0.1 copy.14
  97.0 0.1 broadcast_bitcast_fusion.1
  97.1 0.1 copy.15
  97.4 0.7 slice.38
  98.1 0.2 reduce_sum.27
  98.4 0.2 bitcast_subtract_fusion
  98.6 2.0 fusion.28
  100.6 0.6 copy-done.2
  101.2 2.2 collective-permute-start.2
  103.5 3.6 collective-permute-start.3
  107.1 40.7 %all-to-all-done.1 = f32[32,32,512]{2,1,0:T(8,128)} async-done(((f32[32,32,512]{2,1,0:T(8,128)}), f32[32,32,512]{2,1,0:T(8,128)}, u32[]{:S(2)}, u32[]{:S(2)}) %all-to-all-start.1) | async-done | bytes 2097184 | tf_op jit(solution)/shard_map/all_to_all | solution.py:52
  147.8 5.8 %all-to-all-start.2 = ((f32[32,32,512]{2,1,0:T(8,128)}), f32[32,32,512]{2,1,0:T(8,128)S(1)}, u32[]{:S(2)}, u32[]{:S(2)}) async-start(f32[32,32,512]{2,1,0:T(8,128)} %get-tuple-element.49), calls=%async_computation.2 | async-start | bytes 4194304 | tf_op jit(solution)/shard_map/all_to_all | solution.py:52
  153.5 1.8 reduce_sum.28
  155.3 5.8 %fusion.10.c_ref = f32[512,512]{1,0:T(8,128)S(1)} fusion(f32[32,32,512]{2,1,0:T(8,128)} %all-to-all-done.1, f32[512]{0:T(512)S(1)} %broadcast_multiply_fusion.1, f32[512]{0:T(512)S(1)} %bitcast.97), kind=kOutput, calls=%fused_computation.9 | convolution fusion | flops 3222798336 | bytes 3149824 | tf_op jit(solution)/shard_map/dot_general | solution.py:25
  161.1 25.6 %shard_map.85 = f32[512,512]{1,0:T(8,128)S(1)} custom-call(f32[512,512]{1,0:T(8,128)S(1)} %fusion.10.c_ref), custom_call_target="tpu_custom_call" | custom-call | flops 35999997952 | bytes 2097152 | tf_op jit(solution)/shard_map/pallas_call | solution.py:279
  186.7 2.0 bitcast_subtract_fusion.1
  188.7 0.5 copy-done.3
  189.2 3.9 %bitcast_multiply_fusion = f32[768,512]{1,0:T(8,128)} fusion(f32[1024,768]{1,0:T(8,128)S(1)} %copy-done.3, f32[1024,512]{1,0:T(8,128)S(1)} %bitcast_subtract_fusion.1, f32[6,512]{1,0:T(8,128)S(1)} %pad_maximum_fusion), kind=kOutput, calls=%fused_computation.6 | convolution fusion | flops 2416705536 | bytes 6828032 | tf_op jit(solution)/shard_map/dot_general | solution.py:25
  193.1 0.1 mul.80
  193.2 3.1 fusion.13
  196.4 1.8 fusion.30
  198.2 2.7 fusion.31
  200.9 0.1 mul.84
  201.0 2.9 fusion.14
  204.0 1.8 fusion.32
  205.8 2.7 fusion.33
  208.6 9.8 %all-to-all-start.3 = ((f32[32,32,256]{2,1,0:T(8,128)}), f32[32,32,256]{2,1,0:T(8,128)}, u32[]{:S(2)}, u32[]{:S(2)}) async-start(f32[32,32,256]{2,1,0:T(8,128)} %get-tuple-element.61), calls=%async_computation.3 | async-start | bytes 2097152 | tf_op jit(solution)/shard_map/all_to_all | solution.py:52
  218.5 0.1 copy.16
  218.7 0.6 subtract_bitcast_fusion.in_ref
  219.3 4.1 %fusion.34 = f32[1024,384]{1,0:T(8,128)} fusion(f32[1024,512]{1,0:T(8,128)S(1)} %bitcast.84, f32[512,384]{1,0:T(8,128)} %fusion.31), kind=kOutput, calls=%fused_computation.46 | convolution fusion | flops 1207959552 | bytes 4456448 | tf_op jit(solution)/shard_map/dot_general | solution.py:25
  223.4 3.4 collective-permute-start.4
  226.8 3.0 fusion.35
  229.8 4.0 %collective-permute-start.5 = (f32[1024,384]{1,0:T(8,128)}, f32[1024,384]{1,0:T(8,128)}, u32[]{:S(2)}, u32[]{:S(2)}) collective-permute-start(f32[1024,384]{1,0:T(8,128)} %fusion.35), channel_id=1, source_target_pairs={{8,0},{16,8},{24,16},{56,24},{48,56},{40,48},{32,40},{64,32},{72,6... | collective-permute-start | bytes 4718600 | tf_op jit(solution)/shard_map/ppermute | solution.py:48
  233.9 3.6 fusion.36
  237.5 3.5 fusion.37
  241.0 6.6 %all-to-all-done.3 = f32[32,32,256]{2,1,0:T(8,128)} async-done(((f32[32,32,256]{2,1,0:T(8,128)}), f32[32,32,256]{2,1,0:T(8,128)}, u32[]{:S(2)}, u32[]{:S(2)}) %all-to-all-start.3) | async-done | bytes 1048608 | tf_op jit(solution)/shard_map/all_to_all | solution.py:52
  247.6 1.4 reduce_sum.29
  249.0 3.0 fusion.21
  252.0 4.4 %fusion.38 = f32[1024,256]{1,0:T(8,128)} fusion(f32[512,1024]{1,0:T(8,128)S(1)} %fusion.37, f32[256,512]{1,0:T(8,128)S(1)} %fusion.21), kind=kOutput, calls=%fused_computation.50 | convolution fusion | flops 1610612736 | bytes 3670016 | tf_op jit(solution)/shard_map/dot_general | solution.py:25
  256.4 5.4 %all-to-all-start.4 = ((f32[32,32,256]{2,1,0:T(8,128)}), f32[32,32,256]{2,1,0:T(8,128)S(1)}, u32[]{:S(2)}, u32[]{:S(2)}) async-start(f32[32,32,256]{2,1,0:T(8,128)} %bitcast.87), calls=%async_computation.4 | async-start | bytes 2097152 | tf_op jit(solution)/shard_map/all_to_all | solution.py:52
  261.9 1.2 shard_map.86.starts_ref
  263.1 13.0 %fusion.39.own_ref = f32[1024,768]{1,0:T(8,128)} fusion(f32[512,1024]{1,0:T(8,128)S(1)} %fusion.37, f32[768,512]{1,0:T(8,128)} %bitcast_multiply_fusion), kind=kOutput, calls=%fused_computation.51 | convolution fusion | flops 4831838208 | bytes 6815744 | tf_op jit(solution)/shard_map/dot_general | solution.py:25
  276.0 2.8 shard_map.87.own_ref
  278.9 2.8 shard_map.88
  281.7 7.8 %all-to-all-done.4.mid_ref = f32[32,32,256]{2,1,0:T(8,128)S(1)} async-done(((f32[32,32,256]{2,1,0:T(8,128)}), f32[32,32,256]{2,1,0:T(8,128)S(1)}, u32[]{:S(2)}, u32[]{:S(2)}) %all-to-all-start.4) | async-done | bytes 1048608 | tf_op jit(solution)/shard_map/all_to_all | solution.py:52
  289.5 77.5 %all_to_all.30.rim_ref = f32[32,32,768]{2,1,0:T(8,128)S(1)} all-to-all(f32[32,32,768]{2,1,0:T(8,128)} %bitcast.83), channel_id=1, replica_groups=mesh['member'=32,'region'=8] {'member'}, dimensions={0} | all-to-all | bytes 6291456 | tf_op jit(solution)/shard_map/all_to_all | solution.py:52
  367.0 3.9 %shard_map.89 = f32[32,32768]{1,0:T(8,128)} custom-call(s32[1]{0:T(128)} %bitcast.core_ref, f32[32,32768]{1,0:T(8,128)S(1)} %copy-done.1, f32[32,32,256]{2,1,0:T(8,128)S(1)} %all-to-all-done.4.mid_ref, f32[32,32,768]{2,1,0:T(8,128)S(1)} %all_to_all.30.rim_ref), custom_call_target="tpu_custom_call" | custom-call | flops 1048576 | bytes 12582912 | tf_op jit(solution)/shard_map/pallas_call | solution.py:163
  (37 shorter events, 0.5 us)
Async XLA Ops:
  0.0 2.2 copy-start
  5.9 15.6 %copy-start.8 = (s32[1,32,4]{1,2,0:T(4,128)S(1)}, s32[1,32,4]{1,2,0:T(4,128)}, u32[]{:S(2)}) copy-start(s32[1,32,4]{1,2,0:T(4,128)} %param.13) | copy-start | bytes 1540
  5.9 83.1 %all-to-all-start = ((f32[32,32,768]{2,1,0:T(8,128)}), f32[32,32,768]{2,1,0:T(8,128)S(1)}, u32[]{:S(2)}, u32[]{:S(2)}) async-start(f32[32,32,768]{2,1,0:T(8,128)} %get-tuple-element.42), calls=%async_computation | async-start | bytes 6291456 | tf_op jit(solution)/shard_map/all_to_all | solution.py:52
  19.7 4.8 %collective-permute-start = (f32[72,512]{1,0:T(8,128)}, f32[72,512]{1,0:T(8,128)S(1)}, u32[]{:S(2)}, u32[]{:S(2)}) collective-permute-start(f32[72,512]{1,0:T(8,128)} %get-tuple-element.43), channel_id=1, source_target_pairs={{0,1},{1,2},{2,3},{3,4},{4,5},{5,6},{6,7},{7,0},{8,9},{9,10},{10,1... | collective-permute-start | bytes 442376 | tf_op jit(solution)/shard_map/ppermute | solution.py:324
  19.7 4.8 %collective-permute-start.1 = (f32[72,512]{1,0:T(8,128)}, f32[72,512]{1,0:T(8,128)S(1)}, u32[]{:S(2)}, u32[]{:S(2)}) collective-permute-start(f32[72,512]{1,0:T(8,128)} %get-tuple-element.44), channel_id=1, source_target_pairs={{0,7},{1,0},{2,1},{3,2},{4,3},{5,4},{6,5},{7,6},{8,15},{9,8},{10,9... | collective-permute-start | bytes 442376 | tf_op jit(solution)/shard_map/ppermute | solution.py:325
  24.5 0.7 copy-start.5
  25.1 0.7 copy-start.6
  89.0 7.5 %copy-start.7 = (s32[1,256,4]{1,2,0:T(4,128)S(1)}, s32[1,256,4]{1,2,0:T(4,128)}, u32[]{:S(2)}) copy-start(s32[1,256,4]{1,2,0:T(4,128)} %param.15) | copy-start | bytes 12292
  89.0 58.8 %all-to-all-start.1 = ((f32[32,32,512]{2,1,0:T(8,128)}), f32[32,32,512]{2,1,0:T(8,128)}, u32[]{:S(2)}, u32[]{:S(2)}) async-start(f32[32,32,512]{2,1,0:T(8,128)} %get-tuple-element.46), calls=%async_computation.1 | async-start | bytes 4194304 | tf_op jit(solution)/shard_map/all_to_all | solution.py:52
  98.6 2.7 copy-start.2
  101.2 85.5 %collective-permute-start.2 = (f32[1024,384]{1,0:T(8,128)}, f32[1024,384]{1,0:T(8,128)}, u32[]{:S(2)}, u32[]{:S(2)}) collective-permute-start(f32[1024,384]{1,0:T(8,128)} %get-tuple-element.80), channel_id=1, source_target_pairs={{8,0},{16,8},{24,16},{56,24},{48,56},{40,48},{32,40},{64,32},{72,6... | collective-permute-start | bytes 4718600 | tf_op jit(solution)/shard_map/ppermute | solution.py:48
  103.5 83.3 %collective-permute-start.3 = (f32[1024,384]{1,0:T(8,128)}, f32[1024,384]{1,0:T(8,128)}, u32[]{:S(2)}, u32[]{:S(2)}) collective-permute-start(f32[1024,384]{1,0:T(8,128)} %get-tuple-element.79), channel_id=1, source_target_pairs={{0,8},{8,16},{16,24},{24,56},{56,48},{48,40},{40,32},{32,64},{64,7... | collective-permute-start | bytes 4718600 | tf_op jit(solution)/shard_map/ppermute | solution.py:48
  147.8 60.8 %all-to-all-start.2 = ((f32[32,32,512]{2,1,0:T(8,128)}), f32[32,32,512]{2,1,0:T(8,128)S(1)}, u32[]{:S(2)}, u32[]{:S(2)}) async-start(f32[32,32,512]{2,1,0:T(8,128)} %get-tuple-element.49), calls=%async_computation.2 | async-start | bytes 4194304 | tf_op jit(solution)/shard_map/all_to_all | solution.py:52
  186.7 2.5 copy-start.3
  205.8 12.9 %copy-start.9 = (s32[1,33]{1,0:T(1,128)S(1)}, s32[1,33]{1,0:T(1,128)}, u32[]{:S(2)}) copy-start(s32[1,33]{1,0:T(1,128)} %param.12) | copy-start | bytes 400
  208.6 39.0 %all-to-all-start.3 = ((f32[32,32,256]{2,1,0:T(8,128)}), f32[32,32,256]{2,1,0:T(8,128)}, u32[]{:S(2)}, u32[]{:S(2)}) async-start(f32[32,32,256]{2,1,0:T(8,128)} %get-tuple-element.61), calls=%async_computation.3 | async-start | bytes 2097152 | tf_op jit(solution)/shard_map/all_to_all | solution.py:52
  219.3 7.5 %copy-start.4 = (f32[512,384]{1,0:T(8,128)S(1)}, f32[512,384]{1,0:T(8,128)}, u32[]{:S(2)}) copy-start(f32[512,384]{1,0:T(8,128)} %fusion.33) | copy-start | bytes 2359300
  223.4 52.6 %collective-permute-start.4 = (f32[1024,384]{1,0:T(8,128)}, f32[1024,384]{1,0:T(8,128)}, u32[]{:S(2)}, u32[]{:S(2)}) collective-permute-start(f32[1024,384]{1,0:T(8,128)} %fusion.34), channel_id=1, source_target_pairs={{0,8},{8,16},{16,24},{24,56},{56,48},{48,40},{40,32},{32,64},{64,7... | collective-permute-start | bytes 4718600 | tf_op jit(solution)/shard_map/ppermute | solution.py:48
  229.8 49.0 %collective-permute-start.5 = (f32[1024,384]{1,0:T(8,128)}, f32[1024,384]{1,0:T(8,128)}, u32[]{:S(2)}, u32[]{:S(2)}) collective-permute-start(f32[1024,384]{1,0:T(8,128)} %fusion.35), channel_id=1, source_target_pairs={{8,0},{16,8},{24,16},{56,24},{48,56},{40,48},{32,40},{64,32},{72,6... | collective-permute-start | bytes 4718600 | tf_op jit(solution)/shard_map/ppermute | solution.py:48
  256.4 33.0 %all-to-all-start.4 = ((f32[32,32,256]{2,1,0:T(8,128)}), f32[32,32,256]{2,1,0:T(8,128)S(1)}, u32[]{:S(2)}, u32[]{:S(2)}) async-start(f32[32,32,256]{2,1,0:T(8,128)} %bitcast.87), calls=%async_computation.4 | async-start | bytes 2097152 | tf_op jit(solution)/shard_map/all_to_all | solution.py:52
  289.5 77.5 %copy-start.1 = (f32[32,32768]{1,0:T(8,128)S(1)}, f32[32,32768]{1,0:T(8,128)}, u32[]{:S(2)}) copy-start(f32[32,32768]{1,0:T(8,128)} %x_ref.3) | copy-start | bytes 12582916

commit v4 on v3

--- a/solution.py
+++ b/solution.py
@@ -52,24 +52,35 @@
     return lax.all_to_all(x, "member", split_axis=0, concat_axis=0, tiled=True)
 
 
-def states_kernel(core_ref, x_ref, rim_ref, mid_ref):
-    z = pl.program_id(0)
-    for y in range(COLS):
-        base = place_on_row(z, y, core_ref[0]) * 1024
-        rim_ref[y, :, :384] = x_ref[:, pl.ds(pl.multiple_of(base, 128), 384)]
-        mid_ref[y] = x_ref[:, pl.ds(pl.multiple_of(base + 384, 128), 256)]
-        rim_ref[y, :, 384:] = x_ref[:, pl.ds(pl.multiple_of(base + 640, 128), 384)]
+def states_kernel(core_ref, x_ref, rim_ref, mid_ref, sems):
+    copies = []
+    for z in range(ROWS):
+        for y in range(COLS):
+            base = (z * COLS + place_on_row(z, y, core_ref[0])) * 1024
+            i = z * COLS + y
+            for k, (lo, width, ref, at) in enumerate(
+                ((0, 384, rim_ref, 0), (640, 384, rim_ref, 384), (384, 256, mid_ref, 0))
+            ):
+                copies.append(
+                    pltpu.make_async_copy(
+                        x_ref.at[:, pl.ds(pl.multiple_of(base + lo, 128), width)],
+                        ref.at[i, :, pl.ds(at, width)],
+                        sems.at[i, k],
+                    )
+                )
+                copies[-1].start()
+    for copy in copies:
+        copy.wait()
 
 
 def lay_states(core, x):
     members = x.shape[0]
-    widths = (768, 256)
     return pl.pallas_call(
         states_kernel,
-        grid=(ROWS,),
-        in_specs=[in_smem, pl.BlockSpec((members, 4096), lambda z: (0, z))],
-        out_specs=[pl.BlockSpec((COLS, members, w), lambda z: (z, 0, 0)) for w in widths],
-        out_shape=[jax.ShapeDtypeStruct((ROWS * COLS, members, w), f32) for w in widths],
+        in_specs=[in_smem, in_vmem],
+        out_specs=[pl.BlockSpec(memory_space=pl.ANY)] * 2,
+        out_shape=[jax.ShapeDtypeStruct((ROWS * COLS, members, w), f32) for w in (768, 256)],
+        scratch_shapes=[pltpu.SemaphoreType.DMA((ROWS * COLS, 3))],
         compiler_params=pltpu.CompilerParams(vmem_limit_bytes=16 * 2**20),
         cost_estimate=pl.CostEstimate(flops=0, bytes_accessed=2**23, transcendentals=0),
     )(core, x)
@@ -287,7 +298,7 @@
             pltpu.VMEM((PIECE, PIECE), f32),
         ],
         compiler_params=pltpu.CompilerParams(vmem_limit_bytes=16 * 2**20),
-        cost_estimate=pl.CostEstimate(flops=36 * 10**9, bytes_accessed=2**21, transcendentals=0),
+        cost_estimate=pl.CostEstimate(flops=2 * 10**11, bytes_accessed=2**21, transcendentals=0),
     )(cov)
 
 
@@ -367,14 +378,12 @@
     def solved(g):
         return dot(root, dot(root, g, 1, 1), 0, 0)
 
-    root, rim, head_far, tail_far = in_order(root, rim, head_far, tail_far)
-    rim_gain = gain(rim, jnp.concatenate([cover[3:6], cover[8:11]]))
-    rim_gain, head_far, tail_far = in_order(rim_gain, head_far, tail_far)
+    root, head_far, tail_far = in_order(root, head_far, tail_far)
     head_solved = solved(gain(head_far, cover[11:]))
     tail_solved = solved(gain(tail_far, cover[:3]))
 
-    innov, root, mid_s, rim_gain, head_solved, tail_solved = in_order(
-        innov, root, mid_s, rim_gain, head_solved, tail_solved
+    innov, root, mid_s, head_solved, tail_solved = in_order(
+        innov, root, mid_s, head_solved, tail_solved
     )
     mid = exchange(mid_s)
     innov = whole(innov)
@@ -388,7 +397,8 @@
     mid_inc = dot(weights, gain(centre(whole(mid)), cover[6:8]), 0, 1)
     mid_out = exchange(in_parts(mid_inc))
     mid_inc, starts = in_order(mid_inc, starts)
-    starts, late_weights = in_order(hold(starts), weights)
+    starts, late_weights, rim = in_order(hold(starts), weights, rim)
+    rim_gain = gain(rim, jnp.concatenate([cover[3:6], cover[8:11]]))
     rim_inc = dot(late_weights, rim_gain, 0, 1)
     rim_inc, head_back = in_order(rim_inc, head_back)
     rim_inc = choose(0, starts, rim_inc, head_back)

time: 375 us -> 375 us (level)
  waiting for transfers between devices: 115 us -> 107 us
  matrix products: 59.6 us -> 64.4 us
    all_to_all x5, waiting for transfers between devices: 114 us -> 105 us  [exchange(): return lax.all_to_all(x, 'member', split_axis=0, concat_axis=0, tiled=True)]
    dot_general x15, matrix products: 59.6 us -> 64.4 us  [dot(): lax.dot_general(a, b, (((da,), (db,)), ((), ())), precision=precision, pr...]
  transfers between devices with their start and end apart: 11 -> 11, of which waited for: 5 -> 6; matrix products, arithmetic and copies ran while one was open for 19% -> 21% of each run, Pallas kernels for 10% -> 10%
where the time goes in v4:
time: 375 us; the launch traced here: 371 us
  waiting for transfers between devices  107 us (29%)
  blocking collectives  79.5 us (21%)
  matrix products  64.4 us (17%)
  starting transfers between devices  55.5 us (15%)
  Pallas kernels  45.4 us (12%)
  local copies, waits for them, and re-layouts  11.9 us (3%)
  other arithmetic  6.8 us (2%)
    all_to_all x5, waiting for transfers between devices, exchange(): return lax.all_to_all(x, 'member', split_axis=0, concat_axis=0, tiled=True)  105 us
    all_to_all x1, blocking collectives, exchange(): return lax.all_to_all(x, 'member', split_axis=0, concat_axis=0, tiled=True)  79.5 us
    dot_general x15, matrix products, dot(): lax.dot_general(a, b, (((da,), (db,)), ((), ())), precision=precision, pr...  64.4 us
    all_to_all x5, starting transfers between devices, exchange(): return lax.all_to_all(x, 'member', split_axis=0, concat_axis=0, tiled=True)  40.4 us
    pallas_call x1, Pallas kernels, inverse_factor(): pl.pallas_call(factor_kernel, in_specs=[in_vmem], out_specs=in_vmem, out_...  25.4 us
    ppermute x4, starting transfers between devices, along_snake(): return lax.ppermute(x, BOTH, route)  13.3 us
  transfers between devices with their start and end apart: 11, of which 6 were waited for; matrix products, arithmetic and copies ran while one was open for 21% of the time, Pallas kernels for 10%

profile of v4, /device:TPU:12, one launch (start us, length us, event | category | flops | bytes accessed | tf_op | source)
XLA Modules:
  0.0 370.6 jit_solution(15024350679257886567)
XLA Ops:
  0.0 2.2 copy-done
  2.2 2.8 shard_map.82
  5.0 11.7 %all-to-all-start = ((f32[32,32,768]{2,1,0:T(8,128)}), f32[32,32,768]{2,1,0:T(8,128)S(1)}, u32[]{:S(2)}, u32[]{:S(2)}) async-start(f32[32,32,768]{2,1,0:T(8,128)} %get-tuple-element.38), calls=%async_computation | async-start | bytes 6291456 | tf_op jit(solution)/shard_map/all_to_all | solution.py:52
  16.7 2.0 shard_map.83
  18.7 1.7 collective-permute-start.1
  20.5 0.7 copy.11.lists_ref
  21.2 0.7 pad_add_fusion.place_ref
  21.8 1.7 collective-permute-done.before_ref
  23.5 0.7 copy-done.6
  24.2 0.7 copy-done.7
  24.8 4.5 %shard_map.84 = (f32[32,32,512]{2,1,0:T(8,128)}, f32[32,32,512]{2,1,0:T(8,128)}, f32[8,512]{1,0:T(8,128)}) custom-call(s32[2]{0:T(128)} %pad_add_fusion.place_ref, s32[32,4]{1,0:T(8,128)} %copy.11.lists_ref, f32[32,4096]{1,0:T(8,128)} %pred_ref.3, f32[32,4096]{1,0:T(8,128)} %innov_ref.3, f32[1,4096]{1,0:T(1,128)} %bitcast.89, f32[72,512]{1,0:T(8,128)} %copy-done.6, ...), custom_call_target="tpu_custom_call" | custom-call | bytes 6291456 | tf_op jit(solution)/shard_map/pallas_call | solution.py:148
  29.3 58.7 %all-to-all-done = f32[32,32,768]{2,1,0:T(8,128)S(1)} async-done(((f32[32,32,768]{2,1,0:T(8,128)}), f32[32,32,768]{2,1,0:T(8,128)S(1)}, u32[]{:S(2)}, u32[]{:S(2)}) %all-to-all-start) | async-done | bytes 3145760 | tf_op jit(solution)/shard_map/all_to_all | solution.py:52
  88.0 7.5 %all-to-all-start.1 = ((f32[32,32,512]{2,1,0:T(8,128)}), f32[32,32,512]{2,1,0:T(8,128)}, u32[]{:S(2)}, u32[]{:S(2)}) async-start(f32[32,32,512]{2,1,0:T(8,128)} %get-tuple-element.42), calls=%async_computation.1 | async-start | bytes 4194304 | tf_op jit(solution)/shard_map/all_to_all | solution.py:52
  95.5 0.1 pad_dynamic-slice_fusion
  95.8 0.1 copy.12
  95.9 0.6 copy.28
  96.5 0.1 copy.13
  96.7 0.6 copy.27
  97.3 0.1 copy.14
  97.5 0.6 copy.29
  98.1 0.1 copy.16
  98.2 0.7 copy.15
  98.8 0.7 broadcast_bitcast_fusion
  99.5 0.7 slice.38
  100.2 0.2 reduce_sum.27
  100.5 0.2 bitcast_subtract_fusion
  100.7 2.1 fusion.28
  102.8 0.6 copy-done.2
  103.3 2.2 collective-permute-start.2
  105.6 3.6 collective-permute-start.3
  109.2 37.6 %all-to-all-done.1 = f32[32,32,512]{2,1,0:T(8,128)} async-done(((f32[32,32,512]{2,1,0:T(8,128)}), f32[32,32,512]{2,1,0:T(8,128)}, u32[]{:S(2)}, u32[]{:S(2)}) %all-to-all-start.1) | async-done | bytes 2097184 | tf_op jit(solution)/shard_map/all_to_all | solution.py:52
  146.8 6.1 %all-to-all-start.2 = ((f32[32,32,512]{2,1,0:T(8,128)}), f32[32,32,512]{2,1,0:T(8,128)}, u32[]{:S(2)}, u32[]{:S(2)}) async-start(f32[32,32,512]{2,1,0:T(8,128)} %get-tuple-element.45), calls=%async_computation.2 | async-start | bytes 4194304 | tf_op jit(solution)/shard_map/all_to_all | solution.py:52
  152.9 1.8 reduce_sum.28
  154.7 5.8 %fusion.10.c_ref = f32[512,512]{1,0:T(8,128)S(1)} fusion(f32[32,32,512]{2,1,0:T(8,128)} %all-to-all-done.1, f32[512]{0:T(512)S(1)} %broadcast_multiply_fusion.1, f32[512]{0:T(512)S(1)} %bitcast.94), kind=kOutput, calls=%fused_computation.9 | convolution fusion | flops 3222798336 | bytes 3149824 | tf_op jit(solution)/shard_map/dot_general | solution.py:25
  160.5 25.4 %shard_map.85 = f32[512,512]{1,0:T(8,128)S(1)} custom-call(f32[512,512]{1,0:T(8,128)S(1)} %fusion.10.c_ref), custom_call_target="tpu_custom_call" | custom-call | flops 199999995904 | bytes 2097152 | tf_op jit(solution)/shard_map/pallas_call | solution.py:290
  185.9 1.8 bitcast_subtract_fusion.1
  187.9 2.8 fusion.13
  190.7 1.8 fusion.30
  192.5 3.0 fusion.31
  195.6 2.8 fusion.14
  198.4 1.8 fusion.32
  200.3 2.7 fusion.33
  203.0 2.2 all-to-all-done.2
  205.2 7.6 %all-to-all-start.3 = ((f32[32,32,256]{2,1,0:T(8,128)}), f32[32,32,256]{2,1,0:T(8,128)}, u32[]{:S(2)}, u32[]{:S(2)}) async-start(f32[32,32,256]{2,1,0:T(8,128)} %get-tuple-element.52), calls=%async_computation.3 | async-start | bytes 2097152 | tf_op jit(solution)/shard_map/all_to_all | solution.py:52
  212.9 0.7 subtract_bitcast_fusion.in_ref
  213.6 4.8 %fusion.34 = f32[1024,384]{1,0:T(8,128)} fusion(f32[1024,512]{1,0:T(8,128)} %bitcast.12, f32[512,384]{1,0:T(8,128)} %fusion.31), kind=kOutput, calls=%fused_computation.46 | convolution fusion | flops 1207959552 | bytes 4456448 | tf_op jit(solution)/shard_map/dot_general | solution.py:25
  218.4 3.4 collective-permute-start.4
  221.8 4.5 %fusion.35 = f32[1024,384]{1,0:T(8,128)} fusion(f32[1024,512]{1,0:T(8,128)} %bitcast.12, f32[512,384]{1,0:T(8,128)S(1)} %copy-done.5), kind=kOutput, calls=%fused_computation.47 | convolution fusion | flops 1207959552 | bytes 4456448 | tf_op jit(solution)/shard_map/dot_general | solution.py:25
  226.3 4.2 %collective-permute-start.5 = (f32[1024,384]{1,0:T(8,128)}, f32[1024,384]{1,0:T(8,128)}, u32[]{:S(2)}, u32[]{:S(2)}) collective-permute-start(f32[1024,384]{1,0:T(8,128)} %fusion.35), channel_id=1, source_target_pairs={{8,0},{16,8},{24,16},{56,24},{48,56},{40,48},{32,40},{64,32},{72,6... | collective-permute-start | bytes 4718600 | tf_op jit(solution)/shard_map/ppermute | solution.py:48
  230.5 5.2 %fusion.36 = f32[512,1024]{1,0:T(8,128)S(1)} fusion(f32[512,512]{1,0:T(8,128)S(1)} %shard_map.85, f32[1024,512]{1,0:T(8,128)} %bitcast.12), kind=kOutput, calls=%fused_computation.48 | convolution fusion | flops 3221225472 | bytes 5242880 | tf_op jit(solution)/shard_map/dot_general | solution.py:25
  235.7 4.8 %fusion.37 = f32[512,1024]{1,0:T(8,128)} fusion(f32[512,512]{1,0:T(8,128)S(1)} %shard_map.85, f32[512,1024]{1,0:T(8,128)S(1)} %fusion.36), kind=kOutput, calls=%fused_computation.49 | convolution fusion | flops 3221225472 | bytes 5242880 | tf_op jit(solution)/shard_map/dot_general | solution.py:25
  240.6 1.2 all-to-all-done.3
  241.8 1.4 reduce_sum.29
  243.2 3.1 fusion.21
  246.4 4.5 %fusion.38 = f32[1024,256]{1,0:T(8,128)} fusion(f32[512,1024]{1,0:T(8,128)S(1)} %copy-done.3, f32[256,512]{1,0:T(8,128)S(1)} %fusion.21), kind=kOutput, calls=%fused_computation.50 | convolution fusion | flops 1610612736 | bytes 3670016 | tf_op jit(solution)/shard_map/dot_general | solution.py:25
  250.9 7.5 %all-to-all-start.4 = ((f32[32,32,256]{2,1,0:T(8,128)}), f32[32,32,256]{2,1,0:T(8,128)S(1)}, u32[]{:S(2)}, u32[]{:S(2)}) async-start(f32[32,32,256]{2,1,0:T(8,128)} %bitcast.84), calls=%async_computation.4 | async-start | bytes 2097152 | tf_op jit(solution)/shard_map/all_to_all | solution.py:52
  258.4 1.2 shard_map.86.starts_ref
  259.6 4.7 %bitcast_multiply_fusion = f32[768,512]{1,0:T(8,128)S(1)} fusion(f32[1024,768]{1,0:T(8,128)} %copy-done.2, f32[1024,512]{1,0:T(8,128)S(1)} %bitcast_subtract_fusion.1, f32[6,512]{1,0:T(8,128)S(1)} %pad_maximum_fusion), kind=kOutput, calls=%fused_computation.6 | convolution fusion | flops 2416705536 | bytes 6828032 | tf_op jit(solution)/shard_map/dot_general | solution.py:25
  264.3 12.0 %fusion.39.own_ref = f32[1024,768]{1,0:T(8,128)} fusion(f32[512,1024]{1,0:T(8,128)S(1)} %copy-done.4, f32[768,512]{1,0:T(8,128)S(1)} %bitcast_multiply_fusion), kind=kOutput, calls=%fused_computation.51 | convolution fusion | flops 4831838208 | bytes 6815744 | tf_op jit(solution)/shard_map/dot_general | solution.py:25
  276.3 2.8 shard_map.87.own_ref
  279.1 2.8 shard_map.88
  281.9 5.1 %all-to-all-done.4.mid_ref = f32[32,32,256]{2,1,0:T(8,128)S(1)} async-done(((f32[32,32,256]{2,1,0:T(8,128)}), f32[32,32,256]{2,1,0:T(8,128)S(1)}, u32[]{:S(2)}, u32[]{:S(2)}) %all-to-all-start.4) | async-done | bytes 1048608 | tf_op jit(solution)/shard_map/all_to_all | solution.py:52
  287.0 79.5 %all_to_all.30.rim_ref = f32[32,32,768]{2,1,0:T(8,128)S(1)} all-to-all(f32[32,32,768]{2,1,0:T(8,128)} %bitcast.83), channel_id=1, replica_groups=mesh['member'=32,'region'=8] {'member'}, dimensions={0} | all-to-all | bytes 6291456 | tf_op jit(solution)/shard_map/all_to_all | solution.py:52
  366.5 3.9 %shard_map.89 = f32[32,32768]{1,0:T(8,128)} custom-call(s32[1]{0:T(128)} %bitcast.core_ref, f32[32,32768]{1,0:T(8,128)S(1)} %copy-done.1, f32[32,32,256]{2,1,0:T(8,128)S(1)} %all-to-all-done.4.mid_ref, f32[32,32,768]{2,1,0:T(8,128)S(1)} %all_to_all.30.rim_ref), custom_call_target="tpu_custom_call" | custom-call | flops 1048576 | bytes 12582912 | tf_op jit(solution)/shard_map/pallas_call | solution.py:174
  (53 shorter events, 0.8 us)
Async XLA Ops:
  0.0 2.2 copy-start
  5.0 15.5 %copy-start.16 = (s32[1,32,4]{1,2,0:T(4,128)S(1)}, s32[1,32,4]{1,2,0:T(4,128)}, u32[]{:S(2)}) copy-start(s32[1,32,4]{1,2,0:T(4,128)} %param.13) | copy-start | bytes 1540
  5.0 83.0 %all-to-all-start = ((f32[32,32,768]{2,1,0:T(8,128)}), f32[32,32,768]{2,1,0:T(8,128)S(1)}, u32[]{:S(2)}, u32[]{:S(2)}) async-start(f32[32,32,768]{2,1,0:T(8,128)} %get-tuple-element.38), calls=%async_computation | async-start | bytes 6291456 | tf_op jit(solution)/shard_map/all_to_all | solution.py:52
  18.7 4.8 %collective-permute-start = (f32[72,512]{1,0:T(8,128)}, f32[72,512]{1,0:T(8,128)S(1)}, u32[]{:S(2)}, u32[]{:S(2)}) collective-permute-start(f32[72,512]{1,0:T(8,128)} %get-tuple-element.39), channel_id=1, source_target_pairs={{0,1},{1,2},{2,3},{3,4},{4,5},{5,6},{6,7},{7,0},{8,9},{9,10},{10,1... | collective-permute-start | bytes 442376 | tf_op jit(solution)/shard_map/ppermute | solution.py:335
  18.7 4.8 %collective-permute-start.1 = (f32[72,512]{1,0:T(8,128)}, f32[72,512]{1,0:T(8,128)S(1)}, u32[]{:S(2)}, u32[]{:S(2)}) collective-permute-start(f32[72,512]{1,0:T(8,128)} %get-tuple-element.40), channel_id=1, source_target_pairs={{0,7},{1,0},{2,1},{3,2},{4,3},{5,4},{6,5},{7,6},{8,15},{9,8},{10,9... | collective-permute-start | bytes 442376 | tf_op jit(solution)/shard_map/ppermute | solution.py:336
  23.5 0.7 copy-start.6
  24.1 0.7 copy-start.7
  88.0 7.5 %copy-start.15 = (s32[1,256,4]{1,2,0:T(4,128)S(1)}, s32[1,256,4]{1,2,0:T(4,128)}, u32[]{:S(2)}) copy-start(s32[1,256,4]{1,2,0:T(4,128)} %param.15) | copy-start | bytes 12292
  88.0 58.8 %all-to-all-start.1 = ((f32[32,32,512]{2,1,0:T(8,128)}), f32[32,32,512]{2,1,0:T(8,128)}, u32[]{:S(2)}, u32[]{:S(2)}) async-start(f32[32,32,512]{2,1,0:T(8,128)} %get-tuple-element.42), calls=%async_computation.1 | async-start | bytes 4194304 | tf_op jit(solution)/shard_map/all_to_all | solution.py:52
  100.7 2.7 copy-start.2
  103.3 82.6 %collective-permute-start.2 = (f32[1024,384]{1,0:T(8,128)}, f32[1024,384]{1,0:T(8,128)}, u32[]{:S(2)}, u32[]{:S(2)}) collective-permute-start(f32[1024,384]{1,0:T(8,128)} %get-tuple-element.72), channel_id=1, source_target_pairs={{8,0},{16,8},{24,16},{56,24},{48,56},{40,48},{32,40},{64,32},{72,6... | collective-permute-start | bytes 4718600 | tf_op jit(solution)/shard_map/ppermute | solution.py:48
  105.6 80.3 %collective-permute-start.3 = (f32[1024,384]{1,0:T(8,128)}, f32[1024,384]{1,0:T(8,128)}, u32[]{:S(2)}, u32[]{:S(2)}) collective-permute-start(f32[1024,384]{1,0:T(8,128)} %get-tuple-element.71), channel_id=1, source_target_pairs={{0,8},{8,16},{16,24},{24,56},{56,48},{48,40},{40,32},{32,64},{64,7... | collective-permute-start | bytes 4718600 | tf_op jit(solution)/shard_map/ppermute | solution.py:48
  146.8 58.5 %all-to-all-start.2 = ((f32[32,32,512]{2,1,0:T(8,128)}), f32[32,32,512]{2,1,0:T(8,128)}, u32[]{:S(2)}, u32[]{:S(2)}) async-start(f32[32,32,512]{2,1,0:T(8,128)} %get-tuple-element.45), calls=%async_computation.2 | async-start | bytes 4194304 | tf_op jit(solution)/shard_map/all_to_all | solution.py:52
  154.7 5.8 %copy-start.12 = (f32[512]{0:T(512)}, f32[512]{0:T(512)S(1)}, u32[]{:S(2)}) copy-start(f32[512]{0:T(512)S(1)} %broadcast_multiply_fusion.1) | copy-start | bytes 6148
  185.9 1.9 copy-start.9
  190.7 4.8 %copy-start.8 = (f32[1,3,4,128]{3,1,2,0:T(4,128)S(1)}, f32[1,3,4,128]{3,1,2,0:T(4,128)}, u32[]{:S(2)}) copy-start(f32[1,3,4,128]{3,1,2,0:T(4,128)} %copy.27) | copy-start | bytes 18436
  200.3 12.6 %copy-start.17 = (s32[1,33]{1,0:T(1,128)S(1)}, s32[1,33]{1,0:T(1,128)}, u32[]{:S(2)}) copy-start(s32[1,33]{1,0:T(1,128)} %param.12) | copy-start | bytes 400
  200.3 13.2 %copy-start.14 = (f32[3,4]{1,0:T(4,128)S(1)}, f32[3,4]{1,0:T(4,128)}, u32[]{:S(2)}) copy-start(f32[3,4]{1,0:T(4,128)} %copy.15) | copy-start | bytes 148
  200.3 13.3 %copy-start.10 = (f32[1,3,4,128]{3,2,1,0:T(4,128)S(1)}, f32[1,3,4,128]{3,2,1,0:T(4,128)}, u32[]{:S(2)}) copy-start(f32[1,3,4,128]{3,2,1,0:T(4,128)} %broadcast_bitcast_fusion) | copy-start | bytes 18436
  205.2 36.5 %all-to-all-start.3 = ((f32[32,32,256]{2,1,0:T(8,128)}), f32[32,32,256]{2,1,0:T(8,128)}, u32[]{:S(2)}, u32[]{:S(2)}) async-start(f32[32,32,256]{2,1,0:T(8,128)} %get-tuple-element.52), calls=%async_computation.3 | async-start | bytes 2097152 | tf_op jit(solution)/shard_map/all_to_all | solution.py:52
  213.6 8.2 %copy-start.5 = (f32[512,384]{1,0:T(8,128)S(1)}, f32[512,384]{1,0:T(8,128)}, u32[]{:S(2)}) copy-start(f32[512,384]{1,0:T(8,128)} %fusion.33) | copy-start | bytes 2359300
  218.4 57.8 %collective-permute-start.4 = (f32[1024,384]{1,0:T(8,128)}, f32[1024,384]{1,0:T(8,128)}, u32[]{:S(2)}, u32[]{:S(2)}) collective-permute-start(f32[1024,384]{1,0:T(8,128)} %fusion.34), channel_id=1, source_target_pairs={{0,8},{8,16},{16,24},{24,56},{56,48},{48,40},{40,32},{32,64},{64,7... | collective-permute-start | bytes 4718600 | tf_op jit(solution)/shard_map/ppermute | solution.py:48
  226.3 52.7 %collective-permute-start.5 = (f32[1024,384]{1,0:T(8,128)}, f32[1024,384]{1,0:T(8,128)}, u32[]{:S(2)}, u32[]{:S(2)}) collective-permute-start(f32[1024,384]{1,0:T(8,128)} %fusion.35), channel_id=1, source_target_pairs={{8,0},{16,8},{24,16},{56,24},{48,56},{40,48},{32,40},{64,32},{72,6... | collective-permute-start | bytes 4718600 | tf_op jit(solution)/shard_map/ppermute | solution.py:48
  235.7 7.5 %copy-start.11 = (f32[1,2,4,128]{3,1,2,0:T(2,128)S(1)}, f32[1,2,4,128]{3,1,2,0:T(2,128)}, u32[]{:S(2)}) copy-start(f32[1,2,4,128]{3,1,2,0:T(2,128)} %copy.29) | copy-start | bytes 12292
  235.7 7.5 %copy-start.13 = (f32[512]{0:T(512)S(1)}, f32[512]{0:T(512)}, u32[]{:S(2)}) copy-start(f32[512]{0:T(512)} %copy-done.12) | copy-start | bytes 6148
  243.2 3.1 copy-start.3
  250.9 36.2 %all-to-all-start.4 = ((f32[32,32,256]{2,1,0:T(8,128)}), f32[32,32,256]{2,1,0:T(8,128)S(1)}, u32[]{:S(2)}, u32[]{:S(2)}) async-start(f32[32,32,256]{2,1,0:T(8,128)} %bitcast.84), calls=%async_computation.4 | async-start | bytes 2097152 | tf_op jit(solution)/shard_map/all_to_all | solution.py:52
  259.6 4.7 %copy-start.4 = (f32[512,1024]{1,0:T(8,128)S(1)}, f32[512,1024]{1,0:T(8,128)}, u32[]{:S(2)}) copy-start(f32[512,1024]{1,0:T(8,128)} %fusion.37) | copy-start | bytes 6291460
  287.0 79.5 %copy-start.1 = (f32[32,32768]{1,0:T(8,128)S(1)}, f32[32,32768]{1,0:T(8,128)}, u32[]{:S(2)}) copy-start(f32[32,32768]{1,0:T(8,128)} %x_ref.3) | copy-start | bytes 12582916
